TPU v7x, 32 devices: a whole 2x2x4 slice. The times are simulated.
32 devices in a mesh: sib: 2 (over core), row: 4 (over y, x), col: 4 (over z).
Axes of the slice: x: 2, y: 2, z: 4, core: 2. Of those that a mesh axis runs over, the one named last changes fastest.
Arguments:
- child_update: bfloat16 [2, 8192, 8192], P('sib', 'row', 'col'), may hold values from -6 to 6
- ext_map: int32 [2, 8192], replicated, may hold values from 0 to 16383, as said below
- diag_inverse: bfloat16 [2, 256, 256], replicated, as said below
Outputs:
- front_out: bfloat16 [16384, 16384], P('row', ('sib', 'col'))
- panel_out: bfloat16 [16384, 512], P('row')
Inputs may be any that keep to these rules, and one draw needn't show every extreme that they name: For each child s, the 8192 values of ext_map[s] are distinct. For each child, the rows of one block of 2048 consecutive child rows land at most 512 times in each group of 2048 consecutive front rows and at most 1024 times in each block of 4096 front rows; both bounds are met in every draw. For each child, every block of 4096 front rows receives exactly 2048 child rows, every group of 2048 exactly half of that. Each diag_inverse[p] is lower triangular with positive diagonal.
All inputs are finite; a program needn't handle non-finite values.
Results may differ from a plain program's by a relative error of at most 0.0064.
Values may be sent and summed in bfloat16 or wider, within the bound.
A program may use at most 256 MiB of HBM per device.

v0:
```python
import jax
import jax.numpy as jnp
from jax import lax
from jax.sharding import PartitionSpec as P

FRONT = 16384
PANEL = 256
NPANEL = 2


def broadcast(shard, axis, root):
    mine = lax.axis_index(axis) == root
    return lax.psum(jnp.where(mine, shard, jnp.zeros_like(shard)), axis)


def child_tables(ext_map, part_count, stride, block_rows):
    target = ext_map // stride
    part_ids = jnp.arange(part_count, dtype=jnp.int32)
    onehot = (target[:, :, None] == part_ids[None, None, :]).astype(jnp.int32)
    before = jnp.cumsum(onehot, axis=1) - onehot
    global_rank = jnp.sum(before * onehot, axis=2)
    starts = jnp.repeat(before[:, ::block_rows, :], block_rows, axis=1)
    local_rank = global_rank - jnp.sum(starts * onehot, axis=2)
    return (target, global_rank, local_rank)


def own_slice(table, side_index, first_row, block_rows):
    picked = lax.dynamic_index_in_dim(table, side_index, 0, keepdims=False)
    return lax.dynamic_slice_in_dim(picked, first_row, block_rows, 0)


def on_device(child_update, ext_map, diag_inverse):
    rows_grid = lax.axis_size("row")
    cols_grid = lax.axis_size("col")
    groups = lax.axis_size("sib") * cols_grid
    child_side = lax.axis_index("sib")
    row_pos = lax.axis_index("row")
    col_pos = lax.axis_index("col")
    group_pos = child_side * cols_grid + col_pos
    block_rows = child_update.shape[1]
    child_total = ext_map.shape[1]
    front_rows = FRONT // rows_grid
    front_cols = FRONT // groups
    mean_load = block_rows // groups
    cap_cols = 2 * mean_load
    cap_rows = 4 * mean_load
    block_ids = jnp.arange(child_total, dtype=jnp.int32) // block_rows
    row_target, row_global, row_local = child_tables(ext_map, rows_grid, front_rows, block_rows)
    col_target, col_global, col_local = child_tables(ext_map, groups, front_cols, block_rows)
    own_target = own_slice(row_target, child_side, row_pos * block_rows, block_rows)
    own_rank = own_slice(row_local, child_side, row_pos * block_rows, block_rows)
    send_rows = jnp.zeros((rows_grid * cap_rows, block_rows), jnp.bfloat16)
    send_rows = send_rows.at[own_target * cap_rows + own_rank].set(child_update[0])
    arrived = lax.all_to_all(
        send_rows.reshape(rows_grid, cap_rows, block_rows),
        "row",
        split_axis=0,
        concat_axis=0,
        tiled=True,
    )
    arrived = arrived.reshape(rows_grid * cap_rows, block_rows)
    slot_full = block_ids[None, :] * cap_rows + row_local
    side_target = lax.dynamic_index_in_dim(row_target, child_side, 0, keepdims=False)
    side_global = lax.dynamic_index_in_dim(row_global, child_side, 0, keepdims=False)
    side_slot = lax.dynamic_index_in_dim(slot_full, child_side, 0, keepdims=False)
    where_to = jnp.where(side_target == row_pos, side_global, block_rows)
    row_picks = jnp.zeros((block_rows,), jnp.int32).at[where_to].set(side_slot, mode="drop")
    held_rows = jnp.take(arrived, row_picks, axis=0)
    held_count = held_rows.shape[0]
    own_ctarget = own_slice(col_target, child_side, col_pos * block_rows, block_rows)
    own_crank = own_slice(col_local, child_side, col_pos * block_rows, block_rows)
    send_cols = jnp.zeros((groups * cap_cols, held_count), jnp.bfloat16)
    send_cols = send_cols.at[own_ctarget * cap_cols + own_crank].set(held_rows.T)
    landed = lax.all_to_all(
        send_cols.reshape(groups, cap_cols, held_count),
        ("sib", "col"),
        split_axis=0,
        concat_axis=0,
        tiled=True,
    )
    landed = landed.reshape(groups * cap_cols, held_count)
    assembled = jnp.zeros((front_cols, front_rows), jnp.float32)
    for sibling in range(2):
        col_here = col_target[sibling] == group_pos
        col_place = jnp.where(col_here, ext_map[sibling] - group_pos * front_cols, front_cols)
        col_source = (sibling * cols_grid + block_ids) * cap_cols + col_local[sibling]
        col_pick = jnp.zeros((front_cols,), jnp.int32).at[col_place].set(col_source, mode="drop")
        col_valid = jnp.zeros((front_cols,), jnp.bool_).at[col_place].set(True, mode="drop")
        row_here = row_target[sibling] == row_pos
        row_place = jnp.where(row_here, ext_map[sibling] - row_pos * front_rows, front_rows)
        row_pick = (
            jnp.zeros((front_rows,), jnp.int32).at[row_place].set(row_global[sibling], mode="drop")
        )
        row_valid = jnp.zeros((front_rows,), jnp.bool_).at[row_place].set(True, mode="drop")
        piece = jnp.take(jnp.take(landed, col_pick, axis=0), row_pick, axis=1)
        keep_mask = col_valid[:, None] & row_valid[None, :]
        assembled = assembled + jnp.where(keep_mask, piece.astype(jnp.float32), 0.0)
    front_block = assembled.T
    contract_last = (((1,), (1,)), ((), ()))
    root_row = group_pos * front_cols // front_rows
    start_row = group_pos * front_cols % front_rows
    factors = []
    for panel_step in range(NPANEL):
        first_col = panel_step * PANEL
        owner_group = first_col // front_cols
        offset = first_col % front_cols
        column = front_block[:, offset : offset + PANEL].astype(jnp.bfloat16)
        column = broadcast(column, ("sib", "col"), owner_group)
        inverse = diag_inverse[panel_step]
        factor = lax.dot_general(
            column, inverse, contract_last, preferred_element_type=jnp.float32
        ).astype(jnp.bfloat16)
        chosen = lax.dynamic_slice_in_dim(factor, start_row, front_cols, 0)
        across = broadcast(chosen, "row", root_row)
        front_block = front_block - lax.dot_general(
            factor, across, contract_last, preferred_element_type=jnp.float32
        )
        factors.append(factor)
    return (front_block.astype(jnp.bfloat16), jnp.concatenate(factors, axis=1))


def solution(mesh):
    placed = (P("sib", "row", "col"), P(), P())
    return jax.shard_map(
        on_device,
        mesh=mesh,
        in_specs=placed,
        out_specs=(P("row", ("sib", "col")), P("row", None)),
        check_vma=False,
    )
```

profile of v0, /device:TPU:0, one launch (start us, length us, event | category | flops | bytes accessed | tf_op | source)
XLA Modules:
  0.0 1156.6 jit_solution(6187837446260745466)
XLA Ops:
  7.2 1.1 and_select_fusion
  8.5 2.4 reduce-window.16
  11.2 0.5 reduce-window.19
  12.8 4.8 reduce-window.14
  17.6 0.5 slice_reduce_fusion
  18.1 0.5 reduce-window.15
  19.9 22.9 %scatter_custom_fusion.2 = bf16[4096,2048]{1,0:T(8,128)(2,1)} fusion(s32[2048]{0:T(1024)S(1)} %bitcast.127, bf16[1,2048,2048]{2,1,0:T(8,128)(2,1)} %param.7, bf16[]{:T(256)} %constant.187.clone.1), kind=kCustom, calls=%fused_computation.19 | custom fusion | bytes 25165826 | tf_op jit(solution)/shard_map/scatter | solution.py:53
  42.8 7.1 all-to-all-start
  50.3 30.9 %scatter_custom_fusion.3 = s32[2048]{0:T(1024)S(1)} fusion(s32[8192]{0:T(1024)S(1)} %bitcast.124, s32[8192]{0:T(1024)S(1)} %bitcast.113, s32[]{:T(128)} %constant.173.clone.1), kind=kCustom, calls=%fused_computation.126 | custom fusion | bytes 8196 | tf_op jit(solution)/shard_map/scatter | solution.py:67
  81.2 152.4 %all-to-all-done = bf16[4,1024,2048]{2,1,0:T(8,128)(2,1)} async-done(((bf16[4,1024,2048]{2,1,0:T(8,128)(2,1)}), bf16[4,1024,2048]{2,1,0:T(8,128)(2,1)}, u32[]{:S(2)}, u32[]{:S(2)}) %all-to-all-start) | async-done | bytes 16777248 | tf_op jit(solution)/shard_map/all_to_all | solution.py:54
  233.6 24.2 %gather_fusion = bf16[2048,2048]{1,0:T(8,128)(2,1)} fusion(bf16[4096,2048]{1,0:T(8,128)(2,1)} %bitcast.17, s32[2048]{0:T(1024)S(1)} %fusion.37), kind=kCustom, calls=%fused_computation.clone | custom fusion | bytes 16785408 | tf_op jit(solution)/shard_map/jit(_take)/gather | solution.py:68
  257.9 7.6 select_bitcast_fusion
  265.5 12.3 %copy.19 = bf16[2048,2048]{1,0:T(8,128)(2,1)} copy(bf16[2048,2048]{0,1:T(8,128)(2,1)} %select_bitcast_fusion) | data formatting | bytes 16777216 | tf_op jit(solution)/shard_map/transpose | solution.py:73
  277.8 22.8 %scatter_custom_fusion.4 = bf16[4096,2048]{1,0:T(8,128)(2,1)} fusion(s32[2048]{0:T(1024)S(1)} %bitcast.126, bf16[2048,2048]{1,0:T(8,128)(2,1)} %copy.19, bf16[]{:T(256)} %constant.187.clone.1), kind=kCustom, calls=%fused_computation.22 | custom fusion | bytes 16777728 | tf_op jit(solution)/shard_map/scatter | solution.py:73
  300.6 5.8 all-to-all-start.1
  306.5 30.5 %scatter_custom_fusion.6 = s32[4096]{0:T(1024)S(1)} fusion(s32[8192]{0:T(1024)S(1)} %bitcast.122, s32[8192]{0:T(1024)S(1)} %bitcast.115, s32[]{:T(128)} %constant.173.clone.1), kind=kCustom, calls=%fused_computation.110 | custom fusion | bytes 16388 | tf_op jit(solution)/shard_map/scatter | solution.py:92
  337.0 34.8 %scatter_custom_fusion.1 = pred[4096]{0:T(1024)(128)(4,1)S(1)} fusion(s32[8192]{0:T(1024)S(1)} %bitcast.123, pred[8192]{0:T(1024)(128)(4,1)S(1)} %broadcast.389, pred[]{:T(512)} %constant.171.clone.1), kind=kCustom, calls=%fused_computation.117 | custom fusion | bytes 4097 | tf_op jit(solution)/shard_map/scatter | solution.py:94
  371.8 34.6 %scatter_custom_fusion.8 = pred[4096]{0:T(1024)(128)(4,1)S(1)} fusion(s32[8192]{0:T(1024)S(1)} %bitcast.120, pred[8192]{0:T(1024)(128)(4,1)S(1)} %broadcast.389, pred[]{:T(512)} %constant.171.clone.1), kind=kCustom, calls=%fused_computation.115 | custom fusion | bytes 4097 | tf_op jit(solution)/shard_map/scatter | solution.py:94
  406.4 30.5 %scatter_custom_fusion.10 = s32[4096]{0:T(1024)S(1)} fusion(s32[8192]{0:T(1024)S(1)} %bitcast.121, s32[8192]{0:T(1024)S(1)} %bitcast.114, s32[]{:T(128)} %constant.173.clone.1), kind=kCustom, calls=%fused_computation.108 | custom fusion | bytes 16388 | tf_op jit(solution)/shard_map/scatter | solution.py:92
  436.9 35.0 %scatter_custom_fusion.7 = pred[2048]{0:T(1024)(128)(4,1)S(1)} fusion(s32[8192]{0:T(1024)S(1)} %bitcast.116, pred[8192]{0:T(1024)(128)(4,1)S(1)} %broadcast.389, pred[]{:T(512)} %constant.171.clone.1), kind=kCustom, calls=%fused_computation.128 | custom fusion | bytes 2049 | tf_op jit(solution)/shard_map/scatter | solution.py:88
  471.9 34.6 %scatter_custom_fusion = pred[2048]{0:T(1024)(128)(4,1)S(1)} fusion(s32[8192]{0:T(1024)S(1)} %bitcast.118, pred[8192]{0:T(1024)(128)(4,1)S(1)} %broadcast.389, pred[]{:T(512)} %constant.171.clone.1), kind=kCustom, calls=%fused_computation.130 | custom fusion | bytes 2049 | tf_op jit(solution)/shard_map/scatter | solution.py:88
  506.6 30.4 %scatter_custom_fusion.5 = s32[2048]{0:T(1024)S(1)} fusion(s32[8192]{0:T(1024)S(1)} %bitcast.119, s32[8192]{0:T(1024)S(1)} %fusion.18, s32[]{:T(128)} %constant.173.clone.1), kind=kCustom, calls=%fused_computation.124 | custom fusion | bytes 8196 | tf_op jit(solution)/shard_map/scatter | solution.py:87
  537.0 30.4 %scatter_custom_fusion.9 = s32[2048]{0:T(1024)S(1)} fusion(s32[8192]{0:T(1024)S(1)} %bitcast.117, s32[8192]{0:T(1024)S(1)} %fusion.20, s32[]{:T(128)} %constant.173.clone.1), kind=kCustom, calls=%fused_computation.122 | custom fusion | bytes 8196 | tf_op jit(solution)/shard_map/scatter | solution.py:87
  567.6 102.0 %all-to-all-done.1 = bf16[8,512,2048]{2,1,0:T(8,128)(2,1)} async-done(((bf16[8,512,2048]{2,1,0:T(8,128)(2,1)}), bf16[8,512,2048]{2,1,0:T(8,128)(2,1)}, u32[]{:S(2)}, u32[]{:S(2)}) %all-to-all-start.1) | async-done | bytes 16777248 | tf_op jit(solution)/shard_map/all_to_all | solution.py:74
  669.6 24.4 %gather_fusion.3 = bf16[2048,2048]{1,0:T(8,128)(2,1)} fusion(bf16[4096,2048]{1,0:T(8,128)(2,1)} %bitcast.20, s32[2048]{0:T(1024)S(1)} %fusion.39), kind=kCustom, calls=%fused_computation.3.clone | custom fusion | bytes 16785408 | tf_op jit(solution)/shard_map/jit(_take)/gather | solution.py:95
  694.0 24.2 %gather_fusion.1 = bf16[2048,2048]{1,0:T(8,128)(2,1)} fusion(bf16[4096,2048]{1,0:T(8,128)(2,1)} %bitcast.20, s32[2048]{0:T(1024)S(1)} %fusion.38), kind=kCustom, calls=%fused_computation.2.clone | custom fusion | bytes 16785408 | tf_op jit(solution)/shard_map/jit(_take)/gather | solution.py:95
  718.2 7.6 broadcast_select_fusion
  725.9 12.3 %copy.21 = bf16[2048,2048]{0,1:T(8,128)(2,1)} copy(bf16[2048,2048]{1,0:T(8,128)(2,1)} %broadcast_select_fusion) | data formatting | bytes 16777216 | tf_op jit(solution)/shard_map/jit(_take)/select_n | solution.py:95
  738.2 7.6 broadcast_select_fusion.1
  745.8 12.3 %copy.20 = bf16[2048,2048]{0,1:T(8,128)(2,1)} copy(bf16[2048,2048]{1,0:T(8,128)(2,1)} %broadcast_select_fusion.1) | data formatting | bytes 16777216 | tf_op jit(solution)/shard_map/jit(_take)/select_n | solution.py:95
  758.1 35.8 %gather_fusion.2 = bf16[4096,2048]{1,0:T(8,128)(2,1)} fusion(bf16[2048,2048]{0,1:T(8,128)(2,1)} %copy.20, s32[4096]{0:T(1024)S(1)} %fusion.27), kind=kCustom, calls=%fused_computation.1.clone | custom fusion | bytes 33570816 | tf_op jit(solution)/shard_map/jit(_take)/gather | solution.py:95
  793.9 35.8 %gather_fusion.4 = bf16[4096,2048]{1,0:T(8,128)(2,1)} fusion(bf16[2048,2048]{0,1:T(8,128)(2,1)} %copy.21, s32[4096]{0:T(1024)S(1)} %fusion.28), kind=kCustom, calls=%fused_computation.4.clone | custom fusion | bytes 33570816 | tf_op jit(solution)/shard_map/jit(_take)/gather | solution.py:95
  829.7 19.9 %add_bitcast_fusion = f32[4096,2048]{1,0:T(8,128)S(1)} fusion(bf16[4096,2048]{1,0:T(8,128)(2,1)} %gather_fusion.4, bf16[4096,2048]{1,0:T(8,128)(2,1)} %gather_fusion.2, pred[4096]{0:T(1024)(128)(4,1)S(1)} %get-tuple-element.29, pred[4096]{0:T(1024)(128)(4,1)S(1)} %get-tuple-element.30, pred[2048]{0:T(1024)(128)(4,1)S(1)} %scatter_custom_fusion.7, ...), kind=kLoop, calls=%fused_computation.17 | loop fusion | flops 75497472 | bytes 67129344 | tf_op jit(solution)/shard_map/transpose | solution.py:98
  849.6 11.1 copy-done
  860.6 1.6 fusion.5
  862.3 62.6 %all-reduce.5.cloned.1.call-done = bf16[4096,256]{1,0:T(8,128)(2,1)} async-done(((bf16[4096,256]{1,0:T(8,128)(2,1)}), bf16[4096,256]{1,0:T(8,128)(2,1)}) %all-reduce.5.cloned.1.call-update) | async-done | bytes 2097168 | tf_op jit(solution)/shard_map/psum | solution.py:13
  925.0 2.3 convolution_convert_fusion.1
  927.3 1.4 dynamic-slice_select_fusion.1
  928.8 52.3 %all-reduce.7.cloned.1.call-done = bf16[2048,256]{0,1:T(8,128)(2,1)} async-done(((bf16[2048,256]{0,1:T(8,128)(2,1)}), bf16[2048,256]{0,1:T(8,128)(2,1)}) %all-reduce.7.cloned.1.call-update) | async-done | bytes 1048592 | tf_op jit(solution)/shard_map/psum | solution.py:13
  981.1 25.0 %convolution_subtract_fusion = f32[4096,2048]{1,0:T(8,128)} fusion(f32[4096,2048]{1,0:T(8,128)} %copy-done, bf16[4096,256]{0,1:T(8,128)(2,1)S(1)} %convolution_convert_fusion.1, bf16[2048,256]{0,1:T(8,128)(2,1)} %all-reduce.7.cloned.1.call-done), kind=kOutput, calls=%fused_computation.18 | convolution fusion | flops 4303355904 | bytes 70254592 | tf_op jit(solution)/shard_map/dot_general | solution.py:115
  1006.0 3.7 fusion.6
  1009.8 65.0 %all-reduce.9.cloned.1.call-done = bf16[4096,256]{1,0:T(8,128)(2,1)} async-done(((bf16[4096,256]{1,0:T(8,128)(2,1)}), bf16[4096,256]{1,0:T(8,128)(2,1)}) %all-reduce.9.cloned.1.call-update) | async-done | bytes 2097168 | tf_op jit(solution)/shard_map/psum | solution.py:13
  1074.8 2.3 convolution_convert_fusion
  1077.1 1.2 dynamic-slice_select_fusion
  1078.4 4.0 pad_maximum_fusion
  1082.3 6.4 copy.22
  1088.8 42.0 %all-reduce.11.cloned.1.call-done = bf16[2048,256]{0,1:T(8,128)(2,1)} async-done(((bf16[2048,256]{0,1:T(8,128)(2,1)}), bf16[2048,256]{0,1:T(8,128)(2,1)}) %all-reduce.11.cloned.1.call-update) | async-done | bytes 1048592 | tf_op jit(solution)/shard_map/psum | solution.py:13
  1130.7 19.1 %subtract_convert_fusion = bf16[4096,2048]{1,0:T(8,128)(2,1)} fusion(f32[4096,2048]{1,0:T(8,128)} %convolution_subtract_fusion, bf16[4096,256]{0,1:T(8,128)(2,1)S(1)} %convolution_convert_fusion, bf16[2048,256]{0,1:T(8,128)(2,1)} %all-reduce.11.cloned.1.call-done), kind=kOutput, calls=%fused_computation.16 | convolution fusion | flops 4311744512 | bytes 53477376 | tf_op jit(solution)/shard_map/dot_general | solution.py:115
  (56 shorter events, 3.6 us)
Async XLA Ops:
  42.7 7.2 copy-start.3
  42.8 190.9 %all-to-all-start = ((bf16[4,1024,2048]{2,1,0:T(8,128)(2,1)}), bf16[4,1024,2048]{2,1,0:T(8,128)(2,1)}, u32[]{:S(2)}, u32[]{:S(2)}) async-start(bf16[4,1024,2048]{2,1,0:T(8,128)(2,1)} %bitcast.101), calls=%async_computation | async-start | bytes 33554432 | tf_op jit(solution)/shard_map/all_to_all | solution.py:54
  300.6 369.0 %all-to-all-start.1 = ((bf16[8,512,2048]{2,1,0:T(8,128)(2,1)}), bf16[8,512,2048]{2,1,0:T(8,128)(2,1)}, u32[]{:S(2)}, u32[]{:S(2)}) async-start(bf16[8,512,2048]{2,1,0:T(8,128)(2,1)} %bitcast.100), calls=%async_computation.1 | async-start | bytes 33554432 | tf_op jit(solution)/shard_map/all_to_all | solution.py:74
  306.4 618.5 %all-reduce.5.cloned.1.call-start = ((), (), s32[]{:S(2)}) async-start(), calls=%async_computation.2 | async-start | bytes 4194304 | tf_op jit(solution)/shard_map/psum | solution.py:13
  829.7 95.3 %copy-start.2 = (bf16[2,256,256]{2,1,0:T(8,128)(2,1)S(1)}, bf16[2,256,256]{2,1,0:T(8,128)(2,1)}, u32[]{:S(2)}) copy-start(bf16[2,256,256]{2,1,0:T(8,128)(2,1)} %param.9) | copy-start | bytes 786436
  849.6 11.1 copy-start
  862.3 118.8 %all-reduce.7.cloned.1.call-start = ((), (), s32[]{:S(2)}) async-start(), calls=%async_computation.3 | async-start | bytes 2097152 | tf_op jit(solution)/shard_map/psum | solution.py:13
  927.3 78.7 %copy-start.1 = (bf16[4096,256]{0,1:T(8,128)(2,1)}, bf16[4096,256]{0,1:T(8,128)(2,1)S(1)}, u32[]{:S(2)}) copy-start(bf16[4096,256]{0,1:T(8,128)(2,1)S(1)} %convolution_convert_fusion.1) | copy-start | bytes 6291460
  928.7 146.1 %all-reduce.9.cloned.1.call-start = ((), (), s32[]{:S(2)}) async-start(), calls=%async_computation.4 | async-start | bytes 4194304 | tf_op jit(solution)/shard_map/psum | solution.py:13
  1009.8 121.0 %all-reduce.11.cloned.1.call-start = ((), (), s32[]{:S(2)}) async-start(), calls=%async_computation.5 | async-start | bytes 2097152 | tf_op jit(solution)/shard_map/psum | solution.py:13
Sparse Core Ops, SparseCore 0:
  862.4 62.5 all-reduce.4
  928.8 52.1 all-reduce.6
  1009.9 64.8 all-reduce.8
  1078.5 52.1 all-reduce.10
where the time goes:
time: 1170 us; the launch traced here: 1160 us
  local copies, waits for them, and re-layouts  538 us (46%)
  waiting for transfers between devices  476 us (41%)
  other arithmetic  65.9 us (6%)
  matrix products  48.8 us (4%)
  between operations  14.5 us (1%)
  starting transfers between devices  13 us (1%)
    psum x4, waiting for transfers between devices, broadcast(): return lax.psum(jnp.where(mine, shard, jnp.zeros_like(shard)), axis)  222 us
    all_to_all x1, waiting for transfers between devices, on_device(): lax.all_to_all(send_rows.reshape(rows_grid, cap_rows, block_rows), 'row',...  152 us
    gather x4, local copies, waits for them, and re-layouts, on_device(): piece = jnp.take(jnp.take(landed, col_pick, axis=0), row_pick, axis=1)  120 us
    all_to_all x1, waiting for transfers between devices, on_device(): lax.all_to_all(send_cols.reshape(groups, cap_cols, held_count), ('sib', '...  102 us
    scatter x2, local copies, waits for them, and re-layouts, on_device(): jnp.zeros((front_cols,), jnp.bool_).at[col_place].set(True, mode='drop')  69.6 us
    scatter x2, local copies, waits for them, and re-layouts, on_device(): jnp.zeros((front_rows,), jnp.bool_).at[row_place].set(True, mode='drop')  69.4 us
    scatter x2, local copies, waits for them, and re-layouts, on_device(): jnp.zeros((front_rows,), jnp.int32).at[row_place]  60.9 us
    scatter x2, local copies, waits for them, and re-layouts, on_device(): jnp.zeros((front_cols,), jnp.int32).at[col_place]  60.9 us
  transfers between devices with their start and end apart: 6, of which 6 were waited for; matrix products, arithmetic and copies ran while one was open for 26% of the time, Pallas kernels for 0%

commit v1 on v0

v1 whole, which is shorter than its diff:
```python
import jax
import jax.numpy as jnp
from jax import lax
from jax.sharding import PartitionSpec as P

FRONT = 16384
PANEL = 256
NPANEL = 2


def broadcast(shard, axis, root):
    mine = lax.axis_index(axis) == root
    return lax.psum(jnp.where(mine, shard, jnp.zeros_like(shard)), axis)


CHUNKS = 2
LAST = (((1,), (1,)), ((), ()))
PLAIN = (((1,), (0,)), ((), ()))


def dot(a, b, dims):
    return lax.dot_general(a, b, dims, preferred_element_type=jnp.float32)


def child_tables(ext_map, part_count, stride, block_rows):
    target = ext_map // stride
    part_ids = jnp.arange(part_count, dtype=jnp.int32)
    onehot = (target[:, :, None] == part_ids[None, None, :]).astype(jnp.int32)
    before = jnp.cumsum(onehot, axis=1) - onehot
    global_rank = jnp.sum(before * onehot, axis=2)
    block_start = before[:, ::block_rows, :]
    starts = jnp.repeat(block_start, block_rows, axis=1)
    local_rank = global_rank - jnp.sum(starts * onehot, axis=2)
    counts = jnp.sum(onehot.reshape(2, -1, block_rows, part_count), axis=2)
    return target, global_rank, local_rank, block_start, counts


def own_slice(table, side_index, first_row, block_rows):
    picked = lax.dynamic_index_in_dim(table, side_index, 0, keepdims=False)
    return lax.dynamic_slice_in_dim(picked, first_row, block_rows, 0)


def at_place(count, place, value):
    here = jnp.arange(count, dtype=jnp.int32)[:, None] == place[None, :]
    return jnp.sum(jnp.where(here, value[None, :] + 1, 0), axis=1) - 1


def hot(count, index):
    return (jnp.arange(count, dtype=jnp.int32)[:, None] == index[None, :]).astype(jnp.bfloat16)


def on_device(child_update, ext_map, diag_inverse):
    rows_grid = lax.axis_size("row")
    cols_grid = lax.axis_size("col")
    groups = lax.axis_size("sib") * cols_grid
    side = lax.axis_index("sib")
    row_pos = lax.axis_index("row")
    col_pos = lax.axis_index("col")
    group_pos = side * cols_grid + col_pos
    update = child_update[0]
    block_rows = child_update.shape[1]
    child_total = ext_map.shape[1]
    front_rows = FRONT // rows_grid
    front_cols = FRONT // groups
    mean_load = block_rows // groups
    cap_cols = 2 * mean_load
    cap_rows = 4 * mean_load // CHUNKS
    held_count = block_rows // CHUNKS
    wide = NPANEL * PANEL
    block_ids = jnp.arange(child_total, dtype=jnp.int32) // block_rows
    row_target, row_global, row_local, row_start, row_counts = child_tables(
        ext_map, rows_grid, front_rows, block_rows
    )
    col_target, _, col_local, _, _ = child_tables(ext_map, groups, front_cols, block_rows)

    own_target = own_slice(row_target, side, row_pos * block_rows, block_rows)
    own_local = own_slice(row_local, side, row_pos * block_rows, block_rows)
    own_global = own_slice(row_global, side, row_pos * block_rows, block_rows)
    own_slot = own_target * cap_rows + own_local // CHUNKS
    row_hot = [
        hot(rows_grid * cap_rows, jnp.where(own_global % CHUNKS == part, own_slot, -1))
        for part in range(CHUNKS)
    ]

    start_here = lax.dynamic_slice_in_dim(
        lax.dynamic_index_in_dim(row_start, side, 0, keepdims=False), row_pos, 1, 1
    )
    count_here = lax.dynamic_slice_in_dim(
        lax.dynamic_index_in_dim(row_counts, side, 0, keepdims=False), row_pos, 1, 1
    )
    slot_ids = jnp.arange(cap_rows, dtype=jnp.int32)[None, :] * CHUNKS
    pack_hot = []
    for part in range(CHUNKS):
        inner = slot_ids + (part - start_here) % CHUNKS
        packed = jnp.where(inner < count_here, (start_here + inner) // CHUNKS, -1)
        pack_hot.append(hot(held_count, packed.reshape(-1)))

    own_cext = own_slice(ext_map, side, col_pos * block_rows, block_rows)
    own_ctarget = own_slice(col_target, side, col_pos * block_rows, block_rows)
    own_crank = own_slice(col_local, side, col_pos * block_rows, block_rows)
    col_hot = hot(groups * cap_cols, own_ctarget * cap_cols + own_crank)

    def exchange(sent, width):
        arrived = lax.all_to_all(
            sent.reshape(rows_grid, cap_rows, width), "row", split_axis=0, concat_axis=0, tiled=True
        )
        return arrived.reshape(rows_grid * cap_rows, width)

    landed = []
    for part in range(CHUNKS):
        sent = dot(row_hot[part], update, PLAIN).astype(jnp.bfloat16)
        arrived = exchange(sent, block_rows)
        held = dot(pack_hot[part], arrived, PLAIN).astype(jnp.bfloat16)
        send_cols = dot(col_hot, held, LAST).astype(jnp.bfloat16)
        got = lax.all_to_all(
            send_cols.reshape(groups, cap_cols, held_count),
            ("sib", "col"),
            split_axis=0,
            concat_axis=0,
            tiled=True,
        )
        landed.append(got.reshape(2, cols_grid * cap_cols, held_count))

    row_place = []
    col_place = []
    for sibling in range(2):
        here = row_target[sibling] == row_pos
        order = (row_global[sibling] % CHUNKS) * held_count + row_global[sibling] // CHUNKS
        row_place.append(
            at_place(
                block_rows,
                jnp.where(here, order, -1),
                ext_map[sibling] - row_pos * front_rows,
            )
        )
        here = col_target[sibling] == group_pos
        col_place.append(
            at_place(
                cols_grid * cap_cols,
                jnp.where(here, block_ids * cap_cols + col_local[sibling], -1),
                ext_map[sibling] - group_pos * front_cols,
            )
        )

    strip = dot(update, hot(wide, own_cext), LAST).astype(jnp.bfloat16)
    strip = lax.psum(strip, "col")
    strips = []
    for part in range(CHUNKS):
        sent = dot(row_hot[part], strip, PLAIN).astype(jnp.bfloat16)
        strips.append(dot(pack_hot[part], exchange(sent, wide), PLAIN).astype(jnp.bfloat16))
    strip = jnp.concatenate(strips, axis=0)
    other = lax.ppermute(strip, "sib", [(0, 1), (1, 0)])
    own_rows = hot(front_rows, jnp.where(side == 0, row_place[0], row_place[1]))
    other_rows = hot(front_rows, jnp.where(side == 0, row_place[1], row_place[0]))
    panels = dot(own_rows, strip, PLAIN) + dot(other_rows, other, PLAIN)

    factors = []
    for step in range(NPANEL):
        column = panels[:, step * PANEL : (step + 1) * PANEL]
        for earlier, factor in enumerate(factors):
            first = step * PANEL
            top = lax.slice_in_dim(factor, first % front_rows, first % front_rows + PANEL, axis=0)
            top = broadcast(top, "row", first // front_rows)
            column = column - dot(factor, top, LAST)
        factors.append(dot(column.astype(jnp.bfloat16), diag_inverse[step], LAST).astype(jnp.bfloat16))
    factor = jnp.concatenate(factors, axis=1)
    root_row = group_pos * front_cols // front_rows
    start_row = group_pos * front_cols % front_rows
    across = broadcast(lax.dynamic_slice_in_dim(factor, start_row, front_cols, 0), "row", root_row)

    col_pick = [hot(front_cols, place) for place in col_place]
    front_block = -dot(factor, across, LAST)
    for part in range(CHUNKS):
        spread = jnp.concatenate(
            [dot(landed[part][s], col_pick[s], (((0,), (1,)), ((), ()))).astype(jnp.bfloat16) for s in range(2)],
            axis=0,
        )
        places = jnp.concatenate(
            [row_place[s][part * held_count : (part + 1) * held_count] for s in range(2)]
        )
        front_block = front_block + dot(hot(front_rows, places), spread, PLAIN)
    return front_block.astype(jnp.bfloat16), factor


def solution(mesh):
    placed = (P("sib", "row", "col"), P(), P())
    return jax.shard_map(
        on_device,
        mesh=mesh,
        in_specs=placed,
        out_specs=(P("row", ("sib", "col")), P("row", None)),
        check_vma=False,
    )
```

time: 1170 us -> 884 us (0.76)
  local copies, waits for them, and re-layouts: 538 us -> 22.2 us
  matrix products: 48.8 us -> 305 us
  waiting for transfers between devices: 476 us -> 449 us
  starting transfers between devices: 13 us -> 31 us
  other arithmetic: 65.9 us -> 53.3 us
    scatter x11 -> x0, local copies, waits for them, and re-layouts: 337 us -> none  [the longest x2 69.6 us: on_device(): jnp.zeros((front_cols,), jnp.bool_).at[col_place].set(True, mode='drop')]
    dot_general x4 -> x22, matrix products: 48.8 us -> 305 us  [dot(): return lax.dot_general(a, b, dims, preferred_element_type=jnp.float32)]
    gather x5 -> x0, local copies, waits for them, and re-layouts: 144 us -> none  [the longest x4 120 us: on_device(): piece = jnp.take(jnp.take(landed, col_pick, axis=0), row_pick, axis=1)]
    psum x4 -> x2, waiting for transfers between devices: 222 us -> 92.6 us  [broadcast(): return lax.psum(jnp.where(mine, shard, jnp.zeros_like(shard)), axis)]
    psum x0 -> x1, waiting for transfers between devices: none -> 84.4 us  [on_device(): strip = lax.psum(strip, 'col')]
    reduce_sum x0 -> x5, other arithmetic: none -> 34 us  [the longest x4 33.6 us: at_place(): return jnp.sum(jnp.where(here, value[None, :] + 1, 0), axis=1) - 1]
    transpose x2 -> x0, other arithmetic: 27.5 us -> none  [the longest x1 19.9 us: on_device(): front_block = assembled.T]
    all_to_all x1 -> x2, waiting for transfers between devices: 102 us -> 127 us  [on_device(): lax.all_to_all(send_cols.reshape(groups, cap_cols, held_count), ('sib', '...]
  transfers between devices with their start and end apart: 6 -> 10, of which waited for: 6 -> 8; matrix products, arithmetic and copies ran while one was open for 26% -> 27% of each run, Pallas kernels for 0% -> 0%
where the time goes in v1:
time: 884 us; the launch traced here: 875 us
  waiting for transfers between devices  449 us (51%)
  matrix products  305 us (35%)
  other arithmetic  53.3 us (6%)
  starting transfers between devices  31 us (4%)
  local copies, waits for them, and re-layouts  22.2 us (3%)
  between operations  14.5 us (2%)
    dot_general x22, matrix products, dot(): return lax.dot_general(a, b, dims, preferred_element_type=jnp.float32)  305 us
    all_to_all x4, waiting for transfers between devices, exchange(): lax.all_to_all(sent.reshape(rows_grid, cap_rows, width), 'row', split_axi...  145 us
    all_to_all x2, waiting for transfers between devices, on_device(): lax.all_to_all(send_cols.reshape(groups, cap_cols, held_count), ('sib', '...  127 us
    psum x2, waiting for transfers between devices, broadcast(): return lax.psum(jnp.where(mine, shard, jnp.zeros_like(shard)), axis)  92.6 us
    psum x1, waiting for transfers between devices, on_device(): strip = lax.psum(strip, 'col')  84.4 us
    reduce_sum x4, other arithmetic, at_place(): return jnp.sum(jnp.where(here, value[None, :] + 1, 0), axis=1) - 1  33.6 us
    all_to_all x4, starting transfers between devices, exchange(): lax.all_to_all(sent.reshape(rows_grid, cap_rows, width), 'row', split_axi...  20.1 us
  transfers between devices with their start and end apart: 10, of which 8 were waited for; matrix products, arithmetic and copies ran while one was open for 27% of the time, Pallas kernels for 0%

profile of v1, /device:TPU:0, one launch (start us, length us, event | category | flops | bytes accessed | tf_op | source)
XLA Modules:
  0.0 875.4 jit_solution(8621246367233046212)
XLA Ops:
  7.2 0.8 dynamic_slice.45
  8.0 9.1 %fusion.67 = bf16[2048,512]{0,1:T(8,128)(2,1)} fusion(bf16[1,2048,2048]{2,1,0:T(8,128)(2,1)} %param.3, s32[2048]{0:T(1024)S(1)} %bitcast.150), kind=kOutput, calls=%fused_computation.89 | convolution fusion | flops 4297064448 | bytes 10493952 | tf_op jit(solution)/shard_map/dot_general | solution.py:22
  17.6 2.4 reduce-window.14
  22.2 84.4 %all-reduce.4.cloned.1.call-done = bf16[2048,512]{0,1:T(8,128)(2,1)} async-done(((bf16[2048,512]{0,1:T(8,128)(2,1)}), bf16[2048,512]{0,1:T(8,128)(2,1)}) %all-reduce.4.cloned.1.call-update) | async-done | bytes 2097168 | tf_op jit(solution)/shard_map/psum | solution.py:146
  106.6 7.3 fusion.63
  113.9 3.6 all-to-all-start.1
  117.5 7.3 fusion.62
  124.9 17.7 %all-to-all-done.1 = bf16[4,512,512]{2,1,0:T(8,128)(2,1)S(1)} async-done(((bf16[4,512,512]{2,1,0:T(8,128)(2,1)}), bf16[4,512,512]{2,1,0:T(8,128)(2,1)S(1)}, u32[]{:S(2)}, u32[]{:S(2)}) %all-to-all-start.1) | async-done | bytes 2097184 | tf_op jit(solution)/shard_map/all_to_all | solution.py:104
  142.6 4.7 all-to-all-start
  147.3 21.0 %fusion.42 = bf16[2048,2048]{1,0:T(8,128)(2,1)} fusion(bf16[1,2048,2048]{2,1,0:T(8,128)(2,1)} %param.3, s32[2048]{0:T(1024)S(1)} %bitcast.147), kind=kOutput, calls=%fused_computation.62 | convolution fusion | flops 17188257792 | bytes 16785408 | tf_op jit(solution)/shard_map/dot_general | solution.py:22
  168.3 3.4 all-to-all-done
  171.7 5.7 all-to-all-start.2
  177.5 4.8 reduce-window.16
  184.4 21.1 %fusion.45 = bf16[2048,2048]{1,0:T(8,128)(2,1)} fusion(bf16[1,2048,2048]{2,1,0:T(8,128)(2,1)} %param.3, s32[2048]{0:T(1024)S(1)} %bitcast.143), kind=kOutput, calls=%fused_computation.63 | convolution fusion | flops 17188257792 | bytes 16785408 | tf_op jit(solution)/shard_map/dot_general | solution.py:22
  205.5 63.7 %all-to-all-done.2 = bf16[4,512,2048]{2,1,0:T(8,128)(2,1)} async-done(((bf16[4,512,2048]{2,1,0:T(8,128)(2,1)}), bf16[4,512,2048]{2,1,0:T(8,128)(2,1)}, u32[]{:S(2)}, u32[]{:S(2)}) %all-to-all-start.2) | async-done | bytes 8388640 | tf_op jit(solution)/shard_map/all_to_all | solution.py:104
  269.2 6.1 all-to-all-start.4
  275.8 11.2 %fusion.134 = bf16[1024,2048]{1,0:T(8,128)(2,1)S(1)} fusion(bf16[2048,2048]{1,0:T(8,128)(2,1)} %bitcast.20, s32[2048]{0:T(1024)S(1)} %fusion.92), kind=kOutput, calls=%fused_computation.76.clone.2 | convolution fusion | flops 8594128896 | bytes 12591104 | tf_op jit(solution)/shard_map/dot_general | solution.py:22
  287.1 19.6 %fusion.48 = bf16[4096,1024]{1,0:T(8,128)(2,1)} fusion(s32[2048]{0:T(1024)S(1)} %bitcast.144, bf16[1024,2048]{1,0:T(8,128)(2,1)S(1)} %fusion.134), kind=kOutput, calls=%fused_computation.64 | convolution fusion | flops 17192452096 | bytes 12591104 | tf_op jit(solution)/shard_map/dot_general | solution.py:22
  306.7 60.4 %all-to-all-done.4 = bf16[4,512,2048]{2,1,0:T(8,128)(2,1)} async-done(((bf16[4,512,2048]{2,1,0:T(8,128)(2,1)}), bf16[4,512,2048]{2,1,0:T(8,128)(2,1)}, u32[]{:S(2)}, u32[]{:S(2)}) %all-to-all-start.4) | async-done | bytes 8388640 | tf_op jit(solution)/shard_map/all_to_all | solution.py:104
  367.1 5.3 all-to-all-start.3
  373.2 8.4 select_reduce_fusion.3
  381.5 8.4 select_reduce_fusion.2
  389.9 8.4 select_reduce_fusion.1
  398.3 11.2 %fusion.137 = bf16[1024,2048]{1,0:T(8,128)(2,1)S(1)} fusion(bf16[2048,2048]{1,0:T(8,128)(2,1)} %bitcast.29, s32[2048]{0:T(1024)S(1)} %fusion.94), kind=kOutput, calls=%fused_computation.75.clone | convolution fusion | flops 8594128896 | bytes 12591104 | tf_op jit(solution)/shard_map/dot_general | solution.py:22
  409.5 19.6 %fusion.49 = bf16[4096,1024]{1,0:T(8,128)(2,1)} fusion(s32[2048]{0:T(1024)S(1)} %bitcast.145, bf16[1024,2048]{1,0:T(8,128)(2,1)S(1)} %fusion.137), kind=kOutput, calls=%fused_computation.65 | convolution fusion | flops 17192452096 | bytes 12591104 | tf_op jit(solution)/shard_map/dot_general | solution.py:22
  429.1 126.7 %all-to-all-done.3 = bf16[8,512,1024]{2,1,0:T(8,128)(2,1)} async-done(((bf16[8,512,1024]{2,1,0:T(8,128)(2,1)}), bf16[8,512,1024]{2,1,0:T(8,128)(2,1)}, u32[]{:S(2)}, u32[]{:S(2)}) %all-to-all-start.3) | async-done | bytes 8388640 | tf_op jit(solution)/shard_map/all_to_all | solution.py:115
  555.8 5.1 all-to-all-start.5
  560.9 2.3 fusion.77
  563.2 3.9 fusion.76
  568.2 10.7 %fusion.2 = f32[4096,512]{1,0:T(8,128)S(1)} fusion(s32[2048]{0:T(1024)S(1)} %get-tuple-element.36, bf16[1024,512]{1,0:T(8,128)(2,1)S(1)} %fusion.77, bf16[1024,512]{1,0:T(8,128)(2,1)} %copy-done.6), kind=kOutput, calls=%fused_computation.16 | convolution fusion | flops 8602517504 | bytes 10493952 | tf_op jit(solution)/shard_map/dot_general | solution.py:22
  578.9 10.8 %fusion.50 = f32[4096,512]{1,0:T(8,128)S(1)} fusion(f32[4096,512]{1,0:T(8,128)S(1)} %fusion.2, bf16[2048,512]{1,0:T(8,128)(2,1)} %collective-permute-done, s32[2048]{0:T(1024)S(1)} %get-tuple-element.35), kind=kOutput, calls=%fused_computation.66 | convolution fusion | flops 8600420352 | bytes 18882560 | tf_op jit(solution)/shard_map/dot_general | solution.py:22
  589.6 3.4 copy-done
  595.2 41.8 %all-reduce.6.cloned.1.call-done = bf16[256,256]{0,1:T(8,128)(2,1)} async-done(((bf16[256,256]{0,1:T(8,128)(2,1)}), bf16[256,256]{0,1:T(8,128)(2,1)}) %all-reduce.6.cloned.1.call-update) | async-done | bytes 131088 | tf_op jit(solution)/shard_map/psum | solution.py:13
  637.0 5.1 convolution_convert_fusion
  642.0 3.1 fusion.74
  645.2 8.5 select_reduce_fusion
  653.7 4.0 pad_maximum_fusion
  657.7 6.4 copy.16
  664.2 50.8 %all-reduce.8.cloned.1.call-done = bf16[2048,512]{0,1:T(8,128)(2,1)} async-done(((bf16[2048,512]{0,1:T(8,128)(2,1)}), bf16[2048,512]{0,1:T(8,128)(2,1)}) %all-reduce.8.cloned.1.call-update) | async-done | bytes 2097168 | tf_op jit(solution)/shard_map/psum | solution.py:13
  715.0 17.2 %fusion.106 = f32[4096,2048]{1,0:T(8,128)} fusion(bf16[2048,512]{0,1:T(8,128)(2,1)} %all-reduce.8.cloned.1.call-done, bf16[4096,256]{0,1:T(8,128)(2,1)} %convolution_convert_fusion, bf16[4096,256]{0,1:T(8,128)(2,1)S(1)} %convolution_convert_fusion.1), kind=kOutput, calls=%fused_computation.219 | convolution fusion | flops 8598323200 | bytes 39845888 | tf_op jit(solution)/shard_map/dot_general | solution.py:22
  732.2 5.2 fusion.110
  737.4 10.5 %fusion.58 = bf16[1024,2048]{1,0:T(8,128)(2,1)} fusion(bf16[2048,1024]{1,0:T(8,128)(2,1)S(1)} %bitcast.118, s32[2048]{0:T(1024)S(1)} %broadcast_add_fusion.2), kind=kOutput, calls=%fused_computation.82 | convolution fusion | flops 8596226048 | bytes 8396800 | tf_op jit(solution)/shard_map/dot_general | solution.py:22
  747.9 3.9 fusion.109
  751.9 10.7 %fusion.59 = bf16[1024,2048]{1,0:T(8,128)(2,1)} fusion(bf16[2048,1024]{1,0:T(8,128)(2,1)S(1)} %bitcast.117, s32[2048]{0:T(1024)S(1)} %broadcast_add_fusion.2), kind=kOutput, calls=%fused_computation.83 | convolution fusion | flops 8596226048 | bytes 8396800 | tf_op jit(solution)/shard_map/dot_general | solution.py:22
  762.6 10.5 %fusion.60 = bf16[1024,2048]{1,0:T(8,128)(2,1)} fusion(bf16[2048,1024]{1,0:T(8,128)(2,1)S(1)} %bitcast.115, s32[2048]{0:T(1024)S(1)} %broadcast_add_fusion.3), kind=kOutput, calls=%fused_computation.84 | convolution fusion | flops 8596226048 | bytes 8396800 | tf_op jit(solution)/shard_map/dot_general | solution.py:22
  773.1 10.9 %fusion.61 = bf16[1024,2048]{1,0:T(8,128)(2,1)} fusion(bf16[2048,1024]{1,0:T(8,128)(2,1)S(1)} %bitcast.116, s32[2048]{0:T(1024)S(1)} %broadcast_add_fusion.3), kind=kOutput, calls=%fused_computation.85 | convolution fusion | flops 8596226048 | bytes 8396800 | tf_op jit(solution)/shard_map/dot_general | solution.py:22
  784.0 40.2 %fusion.4 = f32[4096,2048]{1,0:T(8,128)} fusion(s32[2048]{0:T(1024)S(1)} %pad_add_fusion, bf16[1024,2048]{1,0:T(8,128)(2,1)} %fusion.60, bf16[1024,2048]{1,0:T(8,128)(2,1)} %fusion.58), kind=kOutput, calls=%fused_computation.18 | convolution fusion | flops 34384904192 | bytes 41951232 | tf_op jit(solution)/shard_map/dot_general | solution.py:22
  824.2 44.5 %add_convert_fusion = bf16[4096,2048]{1,0:T(8,128)(2,1)} fusion(f32[4096,2048]{1,0:T(8,128)} %fusion.4, f32[4096,2048]{1,0:T(8,128)} %fusion.106, s32[2048]{0:T(1024)S(1)} %copy-done.12, bf16[1024,2048]{1,0:T(8,128)(2,1)} %fusion.61, bf16[1024,2048]{1,0:T(8,128)(2,1)} %fusion.59), kind=kOutput, calls=%fused_computation.8 | convolution fusion | flops 34418458624 | bytes 92282880 | tf_op jit(solution)/shard_map/dot_general | solution.py:22
  (87 shorter events, 9.2 us)
Async XLA Ops:
  7.2 99.4 %all-reduce.4.cloned.1.call-start = ((), (), s32[]{:S(2)}) async-start(), calls=%async_computation.6 | async-start | bytes 4194304 | tf_op jit(solution)/shard_map/psum | solution.py:146
  8.0 9.2 %copy-start.7 = (s32[2,8192]{1,0:T(2,128)S(1)}, s32[2,8192]{1,0:T(2,128)}, u32[]{:S(2)}) copy-start(s32[2,8192]{1,0:T(2,128)} %param.4) | copy-start | bytes 196612
  17.5 96.4 %copy-start.4 = (s32[2,8192]{1,0:T(2,128)}, s32[2,8192]{1,0:T(2,128)S(1)}, u32[]{:S(2)}) copy-start(s32[2,8192]{1,0:T(2,128)S(1)} %get-tuple-element.34) | copy-start | bytes 196612
  21.4 92.5 %copy-start.9 = (s32[2,8192]{1,0:T(2,128)}, s32[2,8192]{1,0:T(2,128)S(1)}, u32[]{:S(2)}) copy-start(s32[2,8192]{1,0:T(2,128)S(1)} %get-tuple-element.24) | copy-start | bytes 196612
  113.9 28.7 %all-to-all-start.1 = ((bf16[4,512,512]{2,1,0:T(8,128)(2,1)}), bf16[4,512,512]{2,1,0:T(8,128)(2,1)S(1)}, u32[]{:S(2)}, u32[]{:S(2)}) async-start(bf16[4,512,512]{2,1,0:T(8,128)(2,1)} %bitcast.121), calls=%async_computation.1 | async-start | bytes 4194304 | tf_op jit(solution)/shard_map/all_to_all | solution.py:104
  142.6 25.7 %copy-start.2 = (bf16[4,512,512]{2,1,0:T(8,128)(2,1)}, bf16[4,512,512]{2,1,0:T(8,128)(2,1)S(1)}, u32[]{:S(2)}) copy-start(bf16[4,512,512]{2,1,0:T(8,128)(2,1)S(1)} %all-to-all-done.1) | copy-start | bytes 6291460
  142.6 29.1 %all-to-all-start = ((bf16[4,512,512]{2,1,0:T(8,128)(2,1)}), bf16[4,512,512]{2,1,0:T(8,128)(2,1)}, u32[]{:S(2)}, u32[]{:S(2)}) async-start(bf16[4,512,512]{2,1,0:T(8,128)(2,1)} %bitcast.120), calls=%async_computation | async-start | bytes 4194304 | tf_op jit(solution)/shard_map/all_to_all | solution.py:104
  171.7 97.5 %all-to-all-start.2 = ((bf16[4,512,2048]{2,1,0:T(8,128)(2,1)}), bf16[4,512,2048]{2,1,0:T(8,128)(2,1)}, u32[]{:S(2)}, u32[]{:S(2)}) async-start(bf16[4,512,2048]{2,1,0:T(8,128)(2,1)} %bitcast.112), calls=%async_computation.2 | async-start | bytes 16777216 | tf_op jit(solution)/shard_map/all_to_all | solution.py:104
  269.2 97.8 %all-to-all-start.4 = ((bf16[4,512,2048]{2,1,0:T(8,128)(2,1)}), bf16[4,512,2048]{2,1,0:T(8,128)(2,1)}, u32[]{:S(2)}, u32[]{:S(2)}) async-start(bf16[4,512,2048]{2,1,0:T(8,128)(2,1)} %bitcast.114), calls=%async_computation.4 | async-start | bytes 16777216 | tf_op jit(solution)/shard_map/all_to_all | solution.py:104
  367.1 5.3 copy-start.8
  367.1 5.4 copy-start.5
  367.1 5.4 copy-start.10
  367.1 188.7 %all-to-all-start.3 = ((bf16[8,512,1024]{2,1,0:T(8,128)(2,1)}), bf16[8,512,1024]{2,1,0:T(8,128)(2,1)}, u32[]{:S(2)}, u32[]{:S(2)}) async-start(bf16[8,512,1024]{2,1,0:T(8,128)(2,1)} %bitcast.113), calls=%async_computation.3 | async-start | bytes 16777216 | tf_op jit(solution)/shard_map/all_to_all | solution.py:115
  555.8 5.1 copy-start.3
  555.8 192.2 %all-to-all-start.5 = ((bf16[8,512,1024]{2,1,0:T(8,128)(2,1)}), bf16[8,512,1024]{2,1,0:T(8,128)(2,1)}, u32[]{:S(2)}, u32[]{:S(2)}) async-start(bf16[8,512,1024]{2,1,0:T(8,128)(2,1)} %bitcast.111), calls=%async_computation.5 | async-start | bytes 16777216 | tf_op jit(solution)/shard_map/all_to_all | solution.py:115
  560.9 76.1 %all-reduce.6.cloned.1.call-start = ((), (), s32[]{:S(2)}) async-start(), calls=%async_computation.7 | async-start | bytes 262144 | tf_op jit(solution)/shard_map/psum | solution.py:13
  567.2 1.0 copy-start.6
  567.3 11.5 %collective-permute-start = (bf16[2048,512]{1,0:T(8,128)(2,1)S(1)}, bf16[2048,512]{1,0:T(8,128)(2,1)}, u32[]{:S(2)}, u32[]{:S(2)}) collective-permute-start(bf16[2048,512]{1,0:T(8,128)(2,1)S(1)} %pad_maximum_fusion.1), channel_id=1, source_target_pairs={{0,16},{16,0},{1,17},{17,1},{2,18},{18,2},{3,19},{19,3},{4,20},{20... | collective-permute-start | bytes 6291464 | tf_op jit(solution)/shard_map/ppermute | solution.py:152
  578.8 14.2 %copy-start.11 = (bf16[2,256,256]{2,1,0:T(8,128)(2,1)S(1)}, bf16[2,256,256]{2,1,0:T(8,128)(2,1)}, u32[]{:S(2)}) copy-start(bf16[2,256,256]{2,1,0:T(8,128)(2,1)} %param.5) | copy-start | bytes 786436
  589.6 3.4 copy-start
  594.5 120.5 %all-reduce.8.cloned.1.call-start = ((), (), s32[]{:S(2)}) async-start(), calls=%async_computation.8 | async-start | bytes 4194304 | tf_op jit(solution)/shard_map/psum | solution.py:13
  751.9 10.7 %copy-start.1 = (bf16[4,512,1024]{2,1,0:T(8,128)(2,1)S(1)}, bf16[4,512,1024]{2,1,0:T(8,128)(2,1)}, u32[]{:S(2)}) copy-start(bf16[4,512,1024]{2,1,0:T(8,128)(2,1)} %get-tuple-element.20) | copy-start | bytes 12582916
  784.0 40.2 %copy-start.12 = (s32[2048]{0:T(1024)S(1)}, s32[2048]{0:T(1024)}, u32[]{:S(2)}) copy-start(s32[2048]{0:T(1024)} %pad_add_fusion.1) | copy-start | bytes 24580
Sparse Core Ops, SparseCore 0:
  17.3 89.2 all-reduce.3
  594.6 42.3 all-reduce.5
  645.3 69.6 all-reduce.7

commit v2 on v1

--- a/solution.py
+++ b/solution.py
@@ -76,18 +76,22 @@
     own_target = own_slice(row_target, side, row_pos * block_rows, block_rows)
     own_local = own_slice(row_local, side, row_pos * block_rows, block_rows)
     own_global = own_slice(row_global, side, row_pos * block_rows, block_rows)
-    own_slot = own_target * cap_rows + own_local // CHUNKS
+    own_slot = (own_target ^ row_pos) * cap_rows + own_local // CHUNKS
     row_hot = [
         hot(rows_grid * cap_rows, jnp.where(own_global % CHUNKS == part, own_slot, -1))
         for part in range(CHUNKS)
     ]
 
-    start_here = lax.dynamic_slice_in_dim(
-        lax.dynamic_index_in_dim(row_start, side, 0, keepdims=False), row_pos, 1, 1
-    )
-    count_here = lax.dynamic_slice_in_dim(
-        lax.dynamic_index_in_dim(row_counts, side, 0, keepdims=False), row_pos, 1, 1
-    )
+    from_row = jnp.arange(rows_grid, dtype=jnp.int32)[:, None] ^ row_pos
+    chosen = from_row == jnp.arange(rows_grid, dtype=jnp.int32)[None, :]
+
+    def arriving(table):
+        table = lax.dynamic_index_in_dim(table, side, 0, keepdims=False)
+        table = lax.dynamic_slice_in_dim(table, row_pos, 1, 1)[:, 0]
+        return jnp.sum(jnp.where(chosen, table[None, :], 0), axis=1)[:, None]
+
+    start_here = arriving(row_start)
+    count_here = arriving(row_counts)
     slot_ids = jnp.arange(cap_rows, dtype=jnp.int32)[None, :] * CHUNKS
     pack_hot = []
     for part in range(CHUNKS):
@@ -100,16 +104,18 @@
     own_crank = own_slice(col_local, side, col_pos * block_rows, block_rows)
     col_hot = hot(groups * cap_cols, own_ctarget * cap_cols + own_crank)
 
-    def exchange(sent, width):
-        arrived = lax.all_to_all(
-            sent.reshape(rows_grid, cap_rows, width), "row", split_axis=0, concat_axis=0, tiled=True
-        )
-        return arrived.reshape(rows_grid * cap_rows, width)
+    def exchange(sent):
+        blocks = [sent[:cap_rows]]
+        for offset in range(1, rows_grid):
+            pairs = [(here, here ^ offset) for here in range(rows_grid)]
+            block = sent[offset * cap_rows : (offset + 1) * cap_rows]
+            blocks.append(lax.ppermute(block, "row", pairs))
+        return jnp.concatenate(blocks, axis=0)
 
     landed = []
     for part in range(CHUNKS):
         sent = dot(row_hot[part], update, PLAIN).astype(jnp.bfloat16)
-        arrived = exchange(sent, block_rows)
+        arrived = exchange(sent)
         held = dot(pack_hot[part], arrived, PLAIN).astype(jnp.bfloat16)
         send_cols = dot(col_hot, held, LAST).astype(jnp.bfloat16)
         got = lax.all_to_all(
@@ -147,7 +153,7 @@
     strips = []
     for part in range(CHUNKS):
         sent = dot(row_hot[part], strip, PLAIN).astype(jnp.bfloat16)
-        strips.append(dot(pack_hot[part], exchange(sent, wide), PLAIN).astype(jnp.bfloat16))
+        strips.append(dot(pack_hot[part], exchange(sent), PLAIN).astype(jnp.bfloat16))
     strip = jnp.concatenate(strips, axis=0)
     other = lax.ppermute(strip, "sib", [(0, 1), (1, 0)])
     own_rows = hot(front_rows, jnp.where(side == 0, row_place[0], row_place[1]))

time: 884 us -> 739 us (0.84)
  waiting for transfers between devices: 449 us -> 254 us
  starting transfers between devices: 31 us -> 69.8 us
  local copies, waits for them, and re-layouts: 22.2 us -> 31.6 us
    all_to_all x4 -> x0, waiting for transfers between devices: 145 us -> none  [exchange(): lax.all_to_all(sent.reshape(rows_grid, cap_rows, width), 'row', split_axi...]
    psum x1, waiting for transfers between devices: 84.4 us -> 0.02 us  [on_device(): strip = lax.psum(strip, 'col')]
    all_to_all x2, waiting for transfers between devices: 127 us -> 62.6 us  [on_device(): lax.all_to_all(send_cols.reshape(groups, cap_cols, held_count), ('sib', '...]
    ppermute x0 -> x12, starting transfers between devices: none -> 59.1 us  [exchange(): blocks.append(lax.ppermute(block, 'row', pairs))]
    ppermute x0 -> x12, waiting for transfers between devices: none -> 54.6 us  [exchange(): blocks.append(lax.ppermute(block, 'row', pairs))]
    psum x2, waiting for transfers between devices: 92.6 us -> 136 us  [broadcast(): return lax.psum(jnp.where(mine, shard, jnp.zeros_like(shard)), axis)]
    all_to_all x4 -> x0, starting transfers between devices: 20.1 us -> none  [exchange(): lax.all_to_all(sent.reshape(rows_grid, cap_rows, width), 'row', split_axi...]
  transfers between devices with their start and end apart: 10 -> 18, of which waited for: 8 -> 6; matrix products, arithmetic and copies ran while one was open for 27% -> 36% of each run, Pallas kernels for 0% -> 0%
where the time goes in v2:
time: 739 us; the launch traced here: 737 us
  matrix products  312 us (42%)
  waiting for transfers between devices  254 us (34%)
  starting transfers between devices  69.8 us (9%)
  other arithmetic  55.3 us (7%)
  local copies, waits for them, and re-layouts  31.6 us (4%)
  between operations  14.5 us (2%)
    dot_general x22, matrix products, dot(): return lax.dot_general(a, b, dims, preferred_element_type=jnp.float32)  312 us
    psum x2, waiting for transfers between devices, broadcast(): return lax.psum(jnp.where(mine, shard, jnp.zeros_like(shard)), axis)  136 us
    all_to_all x2, waiting for transfers between devices, on_device(): lax.all_to_all(send_cols.reshape(groups, cap_cols, held_count), ('sib', '...  62.6 us
    ppermute x12, starting transfers between devices, exchange(): blocks.append(lax.ppermute(block, 'row', pairs))  59.1 us
    ppermute x12, waiting for transfers between devices, exchange(): blocks.append(lax.ppermute(block, 'row', pairs))  54.6 us
    reduce_sum x4, other arithmetic, at_place(): return jnp.sum(jnp.where(here, value[None, :] + 1, 0), axis=1) - 1  33.6 us
  transfers between devices with their start and end apart: 18, of which 6 were waited for; matrix products, arithmetic and copies ran while one was open for 36% of the time, Pallas kernels for 0%

profile of v2, /device:TPU:0, one launch (start us, length us, event | category | flops | bytes accessed | tf_op | source)
XLA Modules:
  0.0 736.6 jit_solution(6814136316479092995)
XLA Ops:
  8.0 9.1 %fusion.81 = bf16[2048,512]{0,1:T(8,128)(2,1)} fusion(bf16[1,2048,2048]{2,1,0:T(8,128)(2,1)} %param.3, s32[2048]{0:T(1024)S(1)} %bitcast.127), kind=kOutput, calls=%fused_computation.103 | convolution fusion | flops 4297064448 | bytes 10493952 | tf_op jit(solution)/shard_map/dot_general | solution.py:22
  17.6 2.4 reduce-window.14
  22.2 19.7 %fusion.56 = bf16[2048,2048]{1,0:T(8,128)(2,1)S(1)} fusion(bf16[1,2048,2048]{2,1,0:T(8,128)(2,1)} %param.3, s32[2048]{0:T(1024)S(1)} %bitcast.119), kind=kOutput, calls=%fused_computation.76 | convolution fusion | flops 17188257792 | bytes 16785408 | tf_op jit(solution)/shard_map/dot_general | solution.py:22
  42.0 3.5 fusion.147
  45.5 3.9 collective-permute-start.9
  49.9 19.9 %fusion.59 = bf16[2048,2048]{1,0:T(8,128)(2,1)S(1)} fusion(bf16[1,2048,2048]{2,1,0:T(8,128)(2,1)} %param.3, s32[2048]{0:T(1024)S(1)} %bitcast.121), kind=kOutput, calls=%fused_computation.77 | convolution fusion | flops 17188257792 | bytes 16785408 | tf_op jit(solution)/shard_map/dot_general | solution.py:22
  69.9 2.8 fusion.145
  72.7 2.9 collective-permute-start.12
  76.7 4.8 reduce-window.16
  83.8 1.2 compare_select_fusion.1
  85.1 11.1 %collective-permute-done.9 = bf16[512,2048]{1,0:T(8,128)(2,1)} collective-permute-done((bf16[512,2048]{1,0:T(8,128)(2,1)}, bf16[512,2048]{1,0:T(8,128)(2,1)}, u32[]{:S(2)}, u32[]{:S(2)}) %collective-permute-start.9) | collective-permute-done | bytes 2097184 | tf_op jit(solution)/shard_map/ppermute | solution.py:112
  96.2 2.0 collective-permute-start.10
  98.2 43.0 %collective-permute-done.8 = bf16[512,2048]{1,0:T(8,128)(2,1)} collective-permute-done((bf16[512,2048]{1,0:T(8,128)(2,1)}, bf16[512,2048]{1,0:T(8,128)(2,1)}, u32[]{:S(2)}, u32[]{:S(2)}) %collective-permute-start.8) | collective-permute-done | bytes 2097184 | tf_op jit(solution)/shard_map/ppermute | solution.py:112
  141.7 11.2 %fusion.20 = bf16[1024,2048]{1,0:T(8,128)(2,1)S(1)} fusion(bf16[512,2048]{1,0:T(8,128)(2,1)} %collective-permute-done.9, bf16[512,2048]{1,0:T(8,128)(2,1)} %collective-permute-done.8, bf16[512,2048]{1,0:T(8,128)(2,1)} %collective-permute-done.7, bf16[512,2048]{1,0:T(8,128)(2,1)} %get-tuple-element.25, s32[2048]{0:T(1024)S(1)} %fusion.124), kind=kOutput, calls=%fused_computation.38 | convolution fusion | flops 8625586176 | bytes 12591104 | tf_op jit(solution)/shard_map/dot_general | solution.py:22
  152.9 31.1 %fusion.62 = bf16[4096,1024]{1,0:T(8,128)(2,1)} fusion(s32[2048]{0:T(1024)S(1)} %bitcast.123, bf16[1024,2048]{1,0:T(8,128)(2,1)S(1)} %fusion.20), kind=kOutput, calls=%fused_computation.78 | convolution fusion | flops 17192452096 | bytes 12591104 | tf_op jit(solution)/shard_map/dot_general | solution.py:22
  184.0 5.1 all-to-all-start
  189.9 8.4 %select_reduce_fusion.3 = s32[2048]{0:T(1024)S(1)} fusion(s32[8192]{0:T(1024)S(1)} %bitcast.117, s32[8192]{0:T(1024)S(1)} %bitcast.111), kind=kLoop, calls=%fused_computation.6 | loop fusion | flops 50329600 | bytes 73728 | tf_op jit(solution)/shard_map/reduce_sum | solution.py:45
  198.2 8.4 %select_reduce_fusion.2 = s32[2048]{0:T(1024)S(1)} fusion(s32[8192]{0:T(1024)S(1)} %bitcast.116, s32[8192]{0:T(1024)S(1)} %bitcast.110), kind=kLoop, calls=%fused_computation.4 | loop fusion | flops 50329600 | bytes 73728 | tf_op jit(solution)/shard_map/reduce_sum | solution.py:45
  206.6 8.4 %select_reduce_fusion.1 = s32[2048]{0:T(1024)S(1)} fusion(s32[8192]{0:T(1024)S(1)} %bitcast.115, s32[8192]{0:T(1024)S(1)} %bitcast.109), kind=kLoop, calls=%fused_computation.2 | loop fusion | flops 50329600 | bytes 73728 | tf_op jit(solution)/shard_map/reduce_sum | solution.py:45
  215.6 6.4 fusion.77
  223.2 45.1 %collective-permute-start.5 = (bf16[512,512]{1,0:T(8,128)(2,1)S(1)}, bf16[512,512]{1,0:T(8,128)(2,1)S(1)}, u32[]{:S(2)}, u32[]{:S(2)}) collective-permute-start(bf16[512,512]{1,0:T(8,128)(2,1)S(1)} %get-tuple-element.34), channel_id=1, source_target_pairs={{0,12},{4,8},{8,4},{12,0},{1,13},{5,9},{9,5},{13,1},{2,14},{6,10},... | collective-permute-start | bytes 1572872 | tf_op jit(solution)/shard_map/ppermute | solution.py:112
  268.3 4.8 fusion.76
  274.7 2.9 collective-permute-start.2
  277.7 10.9 %fusion.31 = bf16[1024,2048]{1,0:T(8,128)(2,1)S(1)} fusion(bf16[512,2048]{1,0:T(8,128)(2,1)} %collective-permute-done.12, bf16[512,2048]{1,0:T(8,128)(2,1)} %collective-permute-done.11, bf16[512,2048]{1,0:T(8,128)(2,1)} %collective-permute-done.10, bf16[512,2048]{1,0:T(8,128)(2,1)S(1)} %get-tuple-element.19, s32[2048]{0:T(1024)S(1)} %fusion.126), kind=kOutput, calls=%fused_computation.49 | convolution fusion | flops 8625586176 | bytes 12591104 | tf_op jit(solution)/shard_map/dot_general | solution.py:22
  288.6 20.0 %fusion.63 = bf16[4096,1024]{1,0:T(8,128)(2,1)} fusion(s32[2048]{0:T(1024)S(1)} %bitcast.124, bf16[1024,2048]{1,0:T(8,128)(2,1)S(1)} %fusion.31), kind=kOutput, calls=%fused_computation.79 | convolution fusion | flops 17192452096 | bytes 12591104 | tf_op jit(solution)/shard_map/dot_general | solution.py:22
  310.0 62.6 %all-to-all-done = bf16[8,512,1024]{2,1,0:T(8,128)(2,1)} async-done(((bf16[8,512,1024]{2,1,0:T(8,128)(2,1)}), bf16[8,512,1024]{2,1,0:T(8,128)(2,1)}, u32[]{:S(2)}, u32[]{:S(2)}) %all-to-all-start) | async-done | bytes 8388640 | tf_op jit(solution)/shard_map/all_to_all | solution.py:121
  372.6 5.1 all-to-all-start.1
  377.7 3.5 fusion.107
  381.3 3.5 fusion.104
  385.8 10.4 %fusion.2 = f32[4096,512]{1,0:T(8,128)S(1)} fusion(s32[2048]{0:T(1024)S(1)} %get-tuple-element.52, bf16[1024,512]{1,0:T(8,128)(2,1)S(1)} %fusion.107, bf16[1024,512]{1,0:T(8,128)(2,1)} %copy-done.2), kind=kOutput, calls=%fused_computation.16 | convolution fusion | flops 8602517504 | bytes 10493952 | tf_op jit(solution)/shard_map/dot_general | solution.py:22
  396.3 10.8 %fusion.64 = f32[4096,512]{1,0:T(8,128)S(1)} fusion(f32[4096,512]{1,0:T(8,128)S(1)} %fusion.2, bf16[2048,512]{1,0:T(8,128)(2,1)} %collective-permute-done.6, s32[2048]{0:T(1024)S(1)} %get-tuple-element.51), kind=kOutput, calls=%fused_computation.80 | convolution fusion | flops 8600420352 | bytes 18882560 | tf_op jit(solution)/shard_map/dot_general | solution.py:22
  407.1 3.4 copy-done
  412.6 85.5 %all-reduce.6.cloned.1.call-done = bf16[256,256]{0,1:T(8,128)(2,1)} async-done(((bf16[256,256]{0,1:T(8,128)(2,1)}), bf16[256,256]{0,1:T(8,128)(2,1)}) %all-reduce.6.cloned.1.call-update) | async-done | bytes 131088 | tf_op jit(solution)/shard_map/psum | solution.py:13
  498.2 5.1 convolution_convert_fusion
  503.2 3.1 fusion.88
  506.4 8.6 %select_reduce_fusion = s32[2048]{0:T(1024)S(1)} fusion(s32[8192]{0:T(1024)S(1)} %bitcast.114, s32[8192]{0:T(1024)S(1)} %bitcast.108), kind=kLoop, calls=%fused_computation | loop fusion | flops 50329600 | bytes 73728 | tf_op jit(solution)/shard_map/reduce_sum | solution.py:45
  515.0 4.0 pad_maximum_fusion
  519.0 6.4 copy.16
  525.4 50.8 %all-reduce.8.cloned.1.call-done = bf16[2048,512]{0,1:T(8,128)(2,1)} async-done(((bf16[2048,512]{0,1:T(8,128)(2,1)}), bf16[2048,512]{0,1:T(8,128)(2,1)}) %all-reduce.8.cloned.1.call-update) | async-done | bytes 2097168 | tf_op jit(solution)/shard_map/psum | solution.py:13
  576.2 17.2 %fusion.142 = f32[4096,2048]{1,0:T(8,128)} fusion(bf16[2048,512]{0,1:T(8,128)(2,1)} %all-reduce.8.cloned.1.call-done, bf16[4096,256]{0,1:T(8,128)(2,1)} %convolution_convert_fusion, bf16[4096,256]{0,1:T(8,128)(2,1)S(1)} %convolution_convert_fusion.1), kind=kOutput, calls=%fused_computation.255 | convolution fusion | flops 8598323200 | bytes 39845888 | tf_op jit(solution)/shard_map/dot_general | solution.py:22
  593.4 5.2 fusion.146
  598.6 10.5 %fusion.72 = bf16[1024,2048]{1,0:T(8,128)(2,1)} fusion(bf16[2048,1024]{1,0:T(8,128)(2,1)S(1)} %bitcast.98, s32[2048]{0:T(1024)S(1)} %copy-done.10), kind=kOutput, calls=%fused_computation.96 | convolution fusion | flops 8596226048 | bytes 8396800 | tf_op jit(solution)/shard_map/dot_general | solution.py:22
  609.1 3.9 fusion.144
  613.1 10.9 %fusion.73 = bf16[1024,2048]{1,0:T(8,128)(2,1)} fusion(bf16[2048,1024]{1,0:T(8,128)(2,1)S(1)} %bitcast.97, s32[2048]{0:T(1024)S(1)} %copy-done.10), kind=kOutput, calls=%fused_computation.97 | convolution fusion | flops 8596226048 | bytes 8396800 | tf_op jit(solution)/shard_map/dot_general | solution.py:22
  624.0 10.5 %fusion.74 = bf16[1024,2048]{1,0:T(8,128)(2,1)} fusion(bf16[2048,1024]{1,0:T(8,128)(2,1)S(1)} %bitcast.95, s32[2048]{0:T(1024)S(1)} %broadcast_add_fusion.3), kind=kOutput, calls=%fused_computation.98 | convolution fusion | flops 8596226048 | bytes 8396800 | tf_op jit(solution)/shard_map/dot_general | solution.py:22
  634.4 10.7 %fusion.75 = bf16[1024,2048]{1,0:T(8,128)(2,1)} fusion(bf16[2048,1024]{1,0:T(8,128)(2,1)S(1)} %bitcast.96, s32[2048]{0:T(1024)S(1)} %broadcast_add_fusion.3), kind=kOutput, calls=%fused_computation.99 | convolution fusion | flops 8596226048 | bytes 8396800 | tf_op jit(solution)/shard_map/dot_general | solution.py:22
  645.1 40.2 %fusion.4 = f32[4096,2048]{1,0:T(8,128)} fusion(s32[2048]{0:T(1024)S(1)} %pad_add_fusion, bf16[1024,2048]{1,0:T(8,128)(2,1)} %fusion.74, bf16[1024,2048]{1,0:T(8,128)(2,1)} %fusion.72), kind=kOutput, calls=%fused_computation.18 | convolution fusion | flops 34384904192 | bytes 41951232 | tf_op jit(solution)/shard_map/dot_general | solution.py:22
  685.3 44.5 %add_convert_fusion = bf16[4096,2048]{1,0:T(8,128)(2,1)} fusion(f32[4096,2048]{1,0:T(8,128)} %fusion.4, f32[4096,2048]{1,0:T(8,128)} %fusion.142, s32[2048]{0:T(1024)S(1)} %copy-done.11, bf16[1024,2048]{1,0:T(8,128)(2,1)} %fusion.75, bf16[1024,2048]{1,0:T(8,128)(2,1)} %fusion.73), kind=kOutput, calls=%fused_computation.8 | convolution fusion | flops 34418458624 | bytes 92282880 | tf_op jit(solution)/shard_map/dot_general | solution.py:22
  (113 shorter events, 16.7 us)
Async XLA Ops:
  7.2 208.4 %all-reduce.4.cloned.1.call-start = ((), (), s32[]{:S(2)}) async-start(), calls=%async_computation.2 | async-start | bytes 4194304 | tf_op jit(solution)/shard_map/psum | solution.py:152
  8.0 9.2 %copy-start.3 = (s32[2,8192]{1,0:T(2,128)S(1)}, s32[2,8192]{1,0:T(2,128)}, u32[]{:S(2)}) copy-start(s32[2,8192]{1,0:T(2,128)} %param.4) | copy-start | bytes 196612
  22.2 19.7 %copy-start.8 = (s32[1,2048]{1,0:T(1,128)}, s32[1,2048]{1,0:T(1,128)S(1)}, u32[]{:S(2)}) copy-start(s32[1,2048]{1,0:T(1,128)S(1)} %compare_select_fusion.13) | copy-start | bytes 24580
  45.5 50.7 %collective-permute-start.9 = (bf16[512,2048]{1,0:T(8,128)(2,1)}, bf16[512,2048]{1,0:T(8,128)(2,1)}, u32[]{:S(2)}, u32[]{:S(2)}) collective-permute-start(bf16[512,2048]{1,0:T(8,128)(2,1)} %get-tuple-element.26), channel_id=1, source_target_pairs={{0,12},{4,8},{8,4},{12,0},{1,13},{5,9},{9,5},{13,1},{2,14},{6,10},... | collective-permute-start | bytes 6291464 | tf_op jit(solution)/shard_map/ppermute | solution.py:112
  49.4 91.8 %collective-permute-start.8 = (bf16[512,2048]{1,0:T(8,128)(2,1)}, bf16[512,2048]{1,0:T(8,128)(2,1)}, u32[]{:S(2)}, u32[]{:S(2)}) collective-permute-start(bf16[512,2048]{1,0:T(8,128)(2,1)} %get-tuple-element.27), channel_id=1, source_target_pairs={{0,8},{4,12},{8,0},{12,4},{1,9},{5,13},{9,1},{13,5},{2,10},{6,14},... | collective-permute-start | bytes 6291464 | tf_op jit(solution)/shard_map/ppermute | solution.py:112
  49.9 91.8 %collective-permute-start.7 = (bf16[512,2048]{1,0:T(8,128)(2,1)}, bf16[512,2048]{1,0:T(8,128)(2,1)}, u32[]{:S(2)}, u32[]{:S(2)}) collective-permute-start(bf16[512,2048]{1,0:T(8,128)(2,1)} %get-tuple-element.28), channel_id=1, source_target_pairs={{0,4},{4,0},{8,12},{12,8},{1,5},{5,1},{9,13},{13,9},{2,6},{6,2},{1... | collective-permute-start | bytes 6291464 | tf_op jit(solution)/shard_map/ppermute | solution.py:112
  72.7 201.5 %collective-permute-start.12 = (bf16[512,2048]{1,0:T(8,128)(2,1)}, bf16[512,2048]{1,0:T(8,128)(2,1)}, u32[]{:S(2)}, u32[]{:S(2)}) collective-permute-start(bf16[512,2048]{1,0:T(8,128)(2,1)} %get-tuple-element.20), channel_id=1, source_target_pairs={{0,12},{4,8},{8,4},{12,0},{1,13},{5,9},{9,5},{13,1},{2,14},{6,10},... | collective-permute-start | bytes 6291464 | tf_op jit(solution)/shard_map/ppermute | solution.py:112
  75.6 199.1 %collective-permute-start.11 = (bf16[512,2048]{1,0:T(8,128)(2,1)}, bf16[512,2048]{1,0:T(8,128)(2,1)}, u32[]{:S(2)}, u32[]{:S(2)}) collective-permute-start(bf16[512,2048]{1,0:T(8,128)(2,1)} %get-tuple-element.21), channel_id=1, source_target_pairs={{0,8},{4,12},{8,0},{12,4},{1,9},{5,13},{9,1},{13,5},{2,10},{6,14},... | collective-permute-start | bytes 6291464 | tf_op jit(solution)/shard_map/ppermute | solution.py:112
  96.2 181.5 %collective-permute-start.10 = (bf16[512,2048]{1,0:T(8,128)(2,1)}, bf16[512,2048]{1,0:T(8,128)(2,1)}, u32[]{:S(2)}, u32[]{:S(2)}) collective-permute-start(bf16[512,2048]{1,0:T(8,128)(2,1)} %get-tuple-element.22), channel_id=1, source_target_pairs={{0,4},{4,0},{8,12},{12,8},{1,5},{5,1},{9,13},{13,9},{2,6},{6,2},{1... | collective-permute-start | bytes 6291464 | tf_op jit(solution)/shard_map/ppermute | solution.py:112
  184.0 5.1 copy-start.4
  184.0 188.5 %all-to-all-start = ((bf16[8,512,1024]{2,1,0:T(8,128)(2,1)}), bf16[8,512,1024]{2,1,0:T(8,128)(2,1)}, u32[]{:S(2)}, u32[]{:S(2)}) async-start(bf16[8,512,1024]{2,1,0:T(8,128)(2,1)} %bitcast.94), calls=%async_computation | async-start | bytes 16777216 | tf_op jit(solution)/shard_map/all_to_all | solution.py:121
  222.0 46.3 %copy-start.9 = (s32[1,2048]{1,0:T(1,128)S(1)}, s32[1,2048]{1,0:T(1,128)}, u32[]{:S(2)}) copy-start(s32[1,2048]{1,0:T(1,128)} %copy-done.8) | copy-start | bytes 24580
  222.0 46.3 %copy-start.12 = (bf16[2048,512]{0,1:T(8,128)(2,1)S(1)}, bf16[2048,512]{0,1:T(8,128)(2,1)}, u32[]{:S(2)}) copy-start(bf16[2048,512]{0,1:T(8,128)(2,1)} %all-reduce.4.cloned.1.call-done) | copy-start | bytes 6291460
  223.2 85.4 %collective-permute-start.5 = (bf16[512,512]{1,0:T(8,128)(2,1)S(1)}, bf16[512,512]{1,0:T(8,128)(2,1)S(1)}, u32[]{:S(2)}, u32[]{:S(2)}) collective-permute-start(bf16[512,512]{1,0:T(8,128)(2,1)S(1)} %get-tuple-element.34), channel_id=1, source_target_pairs={{0,12},{4,8},{8,4},{12,0},{1,13},{5,9},{9,5},{13,1},{2,14},{6,10},... | collective-permute-start | bytes 1572872 | tf_op jit(solution)/shard_map/ppermute | solution.py:112
  268.2 109.5 %collective-permute-start.4 = (bf16[512,512]{1,0:T(8,128)(2,1)}, bf16[512,512]{1,0:T(8,128)(2,1)}, u32[]{:S(2)}, u32[]{:S(2)}) collective-permute-start(bf16[512,512]{1,0:T(8,128)(2,1)} %get-tuple-element.35), channel_id=1, source_target_pairs={{0,8},{4,12},{8,0},{12,4},{1,9},{5,13},{9,1},{13,5},{2,10},{6,14},... | collective-permute-start | bytes 1572872 | tf_op jit(solution)/shard_map/ppermute | solution.py:112
  274.2 103.5 %collective-permute-start.3 = (bf16[512,512]{1,0:T(8,128)(2,1)}, bf16[512,512]{1,0:T(8,128)(2,1)}, u32[]{:S(2)}, u32[]{:S(2)}) collective-permute-start(bf16[512,512]{1,0:T(8,128)(2,1)} %get-tuple-element.36), channel_id=1, source_target_pairs={{0,4},{4,0},{8,12},{12,8},{1,5},{5,1},{9,13},{13,9},{2,6},{6,2},{1... | collective-permute-start | bytes 1572872 | tf_op jit(solution)/shard_map/ppermute | solution.py:112
  274.7 106.5 %collective-permute-start.2 = (bf16[512,512]{1,0:T(8,128)(2,1)}, bf16[512,512]{1,0:T(8,128)(2,1)}, u32[]{:S(2)}, u32[]{:S(2)}) collective-permute-start(bf16[512,512]{1,0:T(8,128)(2,1)} %get-tuple-element.30), channel_id=1, source_target_pairs={{0,12},{4,8},{8,4},{12,0},{1,13},{5,9},{9,5},{13,1},{2,14},{6,10},... | collective-permute-start | bytes 1572872 | tf_op jit(solution)/shard_map/ppermute | solution.py:112
  277.7 103.6 %collective-permute-start.1 = (bf16[512,512]{1,0:T(8,128)(2,1)}, bf16[512,512]{1,0:T(8,128)(2,1)}, u32[]{:S(2)}, u32[]{:S(2)}) collective-permute-start(bf16[512,512]{1,0:T(8,128)(2,1)} %get-tuple-element.31), channel_id=1, source_target_pairs={{0,8},{4,12},{8,0},{12,4},{1,9},{5,13},{9,1},{13,5},{2,10},{6,14},... | collective-permute-start | bytes 1572872 | tf_op jit(solution)/shard_map/ppermute | solution.py:112
  308.6 0.8 copy-start.13
  309.4 71.9 %collective-permute-start = (bf16[512,512]{1,0:T(8,128)(2,1)}, bf16[512,512]{1,0:T(8,128)(2,1)S(1)}, u32[]{:S(2)}, u32[]{:S(2)}) collective-permute-start(bf16[512,512]{1,0:T(8,128)(2,1)} %get-tuple-element.32), channel_id=1, source_target_pairs={{0,4},{4,0},{8,12},{12,8},{1,5},{5,1},{9,13},{13,9},{2,6},{6,2},{1... | collective-permute-start | bytes 1572872 | tf_op jit(solution)/shard_map/ppermute | solution.py:112
  372.6 5.2 copy-start.14
  372.6 236.6 %all-to-all-start.1 = ((bf16[8,512,1024]{2,1,0:T(8,128)(2,1)}), bf16[8,512,1024]{2,1,0:T(8,128)(2,1)}, u32[]{:S(2)}, u32[]{:S(2)}) async-start(bf16[8,512,1024]{2,1,0:T(8,128)(2,1)} %bitcast.93), calls=%async_computation.1 | async-start | bytes 16777216 | tf_op jit(solution)/shard_map/all_to_all | solution.py:121
  377.7 120.5 %all-reduce.6.cloned.1.call-start = ((), (), s32[]{:S(2)}) async-start(), calls=%async_computation.3 | async-start | bytes 262144 | tf_op jit(solution)/shard_map/psum | solution.py:13
  384.9 1.0 copy-start.2
  385.0 11.3 %collective-permute-start.6 = (bf16[2048,512]{1,0:T(8,128)(2,1)S(1)}, bf16[2048,512]{1,0:T(8,128)(2,1)}, u32[]{:S(2)}, u32[]{:S(2)}) collective-permute-start(bf16[2048,512]{1,0:T(8,128)(2,1)S(1)} %pad_maximum_fusion.1), channel_id=1, source_target_pairs={{0,16},{16,0},{1,17},{17,1},{2,18},{18,2},{3,19},{19,3},{4,20},{20... | collective-permute-start | bytes 6291464 | tf_op jit(solution)/shard_map/ppermute | solution.py:158
  396.3 14.2 %copy-start.5 = (bf16[2,256,256]{2,1,0:T(8,128)(2,1)S(1)}, bf16[2,256,256]{2,1,0:T(8,128)(2,1)}, u32[]{:S(2)}) copy-start(bf16[2,256,256]{2,1,0:T(8,128)(2,1)} %param.5) | copy-start | bytes 786436
  407.1 3.4 copy-start
  412.0 164.2 %all-reduce.8.cloned.1.call-start = ((), (), s32[]{:S(2)}) async-start(), calls=%async_computation.4 | async-start | bytes 4194304 | tf_op jit(solution)/shard_map/psum | solution.py:13
  503.2 3.1 copy-start.6
  503.2 3.1 copy-start.7
  593.4 5.2 copy-start.10
  613.1 10.9 %copy-start.1 = (bf16[4,512,1024]{2,1,0:T(8,128)(2,1)S(1)}, bf16[4,512,1024]{2,1,0:T(8,128)(2,1)}, u32[]{:S(2)}) copy-start(bf16[4,512,1024]{2,1,0:T(8,128)(2,1)} %get-tuple-element.24) | copy-start | bytes 12582916
  645.1 40.2 %copy-start.11 = (s32[2048]{0:T(1024)S(1)}, s32[2048]{0:T(1024)}, u32[]{:S(2)}) copy-start(s32[2048]{0:T(1024)} %pad_add_fusion.1) | copy-start | bytes 24580
Sparse Core Ops, SparseCore 0:
  17.3 89.2 all-reduce.3
  412.1 86.0 all-reduce.5
  506.5 69.6 all-reduce.7

commit v3 on v2

--- a/solution.py
+++ b/solution.py
@@ -150,6 +150,9 @@
 
     strip = dot(update, hot(wide, own_cext), LAST).astype(jnp.bfloat16)
     strip = lax.psum(strip, "col")
+    own_rext = own_slice(ext_map, side, row_pos * block_rows, block_rows)
+    tops = dot(hot(wide, own_rext)[PANEL:], strip[:, : wide - PANEL], PLAIN)
+    tops = lax.psum(tops, ("sib", "row"))
     strips = []
     for part in range(CHUNKS):
         sent = dot(row_hot[part], strip, PLAIN).astype(jnp.bfloat16)
@@ -160,23 +163,26 @@
     other_rows = hot(front_rows, jnp.where(side == 0, row_place[1], row_place[0]))
     panels = dot(own_rows, strip, PLAIN) + dot(other_rows, other, PLAIN)
 
+    top_factors = []
+    for step in range(NPANEL - 1):
+        column = tops[:, step * PANEL : (step + 1) * PANEL]
+        for factor in top_factors:
+            column = column - dot(factor, factor[(step - 1) * PANEL : step * PANEL], LAST)
+        top_factors.append(
+            dot(column.astype(jnp.bfloat16), diag_inverse[step], LAST).astype(jnp.bfloat16)
+        )
     factors = []
     for step in range(NPANEL):
         column = panels[:, step * PANEL : (step + 1) * PANEL]
-        for earlier, factor in enumerate(factors):
-            first = step * PANEL
-            top = lax.slice_in_dim(factor, first % front_rows, first % front_rows + PANEL, axis=0)
-            top = broadcast(top, "row", first // front_rows)
-            column = column - dot(factor, top, LAST)
+        for factor, top in zip(factors, top_factors):
+            column = column - dot(factor, top[(step - 1) * PANEL : step * PANEL], LAST)
         factors.append(dot(column.astype(jnp.bfloat16), diag_inverse[step], LAST).astype(jnp.bfloat16))
     factor = jnp.concatenate(factors, axis=1)
     root_row = group_pos * front_cols // front_rows
     start_row = group_pos * front_cols % front_rows
-    across = broadcast(lax.dynamic_slice_in_dim(factor, start_row, front_cols, 0), "row", root_row)
-
     col_pick = [hot(front_cols, place) for place in col_place]
-    front_block = -dot(factor, across, LAST)
-    for part in range(CHUNKS):
+
+    def placed(part):
         spread = jnp.concatenate(
             [dot(landed[part][s], col_pick[s], (((0,), (1,)), ((), ()))).astype(jnp.bfloat16) for s in range(2)],
             axis=0,
@@ -184,7 +190,16 @@
         places = jnp.concatenate(
             [row_place[s][part * held_count : (part + 1) * held_count] for s in range(2)]
         )
-        front_block = front_block + dot(hot(front_rows, places), spread, PLAIN)
+        return dot(hot(front_rows, places), spread, PLAIN)
+
+    chosen = lax.dynamic_slice_in_dim(factor, start_row, front_cols, 0)
+    across = broadcast(chosen, "row", root_row)
+    front_block = placed(0)
+    across, front_block = lax.optimization_barrier((across, front_block))
+    front_block = front_block - dot(factor, across, LAST)
+    landed[1:], front_block = lax.optimization_barrier((landed[1:], front_block))
+    for part in range(1, CHUNKS):
+        front_block = front_block + placed(part)
     return front_block.astype(jnp.bfloat16), factor
 
 

time: 739 us -> 623 us (0.84)
  waiting for transfers between devices: 254 us -> 156 us
  starting transfers between devices: 69.8 us -> 23.7 us
  blocking collectives: 0 us -> 33 us
    psum x2 -> x1, waiting for transfers between devices: 136 us -> 0.01 us  [broadcast(): return lax.psum(jnp.where(mine, shard, jnp.zeros_like(shard)), axis)]
    ppermute x12, starting transfers between devices: 59.1 us -> 13.3 us  [exchange(): blocks.append(lax.ppermute(block, 'row', pairs))]
    psum x0 -> x1, blocking collectives: none -> 33 us  [on_device(): tops = lax.psum(tops, ('sib', 'row'))]
    all_to_all x2, waiting for transfers between devices: 62.6 us -> 93.7 us  [on_device(): lax.all_to_all(send_cols.reshape(groups, cap_cols, held_count), ('sib', '...]
    dot_general x22 -> x24, matrix products: 312 us -> 305 us  [dot(): return lax.dot_general(a, b, dims, preferred_element_type=jnp.float32)]
  transfers between devices with their start and end apart: 18 -> 17, of which waited for: 6 -> 6; matrix products, arithmetic and copies ran while one was open for 36% -> 47% of each run, Pallas kernels for 0% -> 0%
where the time goes in v3:
time: 623 us; the launch traced here: 615 us
  matrix products  305 us (49%)
  waiting for transfers between devices  156 us (25%)
  other arithmetic  57.1 us (9%)
  blocking collectives  33 us (5%)
  local copies, waits for them, and re-layouts  25.9 us (4%)
  starting transfers between devices  23.7 us (4%)
  between operations  14.9 us (2%)
    dot_general x24, matrix products, dot(): return lax.dot_general(a, b, dims, preferred_element_type=jnp.float32)  305 us
    all_to_all x2, waiting for transfers between devices, on_device(): lax.all_to_all(send_cols.reshape(groups, cap_cols, held_count), ('sib', '...  93.7 us
    ppermute x12, waiting for transfers between devices, exchange(): blocks.append(lax.ppermute(block, 'row', pairs))  61.8 us
    reduce_sum x4, other arithmetic, at_place(): return jnp.sum(jnp.where(here, value[None, :] + 1, 0), axis=1) - 1  33.3 us
    psum x1, blocking collectives, on_device(): tops = lax.psum(tops, ('sib', 'row'))  33 us
    ppermute x12, starting transfers between devices, exchange(): blocks.append(lax.ppermute(block, 'row', pairs))  13.3 us
  transfers between devices with their start and end apart: 17, of which 6 were waited for; matrix products, arithmetic and copies ran while one was open for 47% of the time, Pallas kernels for 0%

profile of v3, /device:TPU:0, one launch (start us, length us, event | category | flops | bytes accessed | tf_op | source)
XLA Modules:
  0.0 614.9 jit_solution(16483975199036026735)
XLA Ops:
  8.5 2.4 reduce-window.16
  12.9 1.6 compare_select_fusion.12
  14.4 19.7 %fusion.59 = bf16[2048,2048]{1,0:T(8,128)(2,1)S(1)} fusion(bf16[1,2048,2048]{2,1,0:T(8,128)(2,1)} %param.3, s32[2048]{0:T(1024)S(1)} %bitcast.135), kind=kOutput, calls=%fused_computation.78 | convolution fusion | flops 17188257792 | bytes 16785408 | tf_op jit(solution)/shard_map/dot_general | solution.py:22
  34.1 4.3 fusion.160
  38.4 2.9 collective-permute-start.10
  42.8 5.8 fusion.89
  48.7 20.2 %fusion.56 = bf16[2048,2048]{1,0:T(8,128)(2,1)S(1)} fusion(bf16[1,2048,2048]{2,1,0:T(8,128)(2,1)} %param.3, s32[2048]{0:T(1024)S(1)} %bitcast.128), kind=kOutput, calls=%fused_computation.77 | convolution fusion | flops 17188257792 | bytes 16785408 | tf_op jit(solution)/shard_map/dot_general | solution.py:22
  68.8 2.8 fusion.161
  71.7 2.0 collective-permute-start
  73.7 1.5 collective-permute-start.1
  75.3 4.8 reduce-window.14
  83.7 8.4 %select_reduce_fusion.1 = s32[2048]{0:T(1024)S(1)} fusion(s32[8192]{0:T(1024)S(1)} %bitcast.126, s32[8192]{0:T(1024)S(1)} %bitcast.120), kind=kLoop, calls=%fused_computation.2 | loop fusion | flops 50329600 | bytes 73728 | tf_op jit(solution)/shard_map/reduce_sum | solution.py:45
  92.6 8.3 %select_reduce_fusion.2 = s32[2048]{0:T(1024)S(1)} fusion(s32[8192]{0:T(1024)S(1)} %bitcast.125, s32[8192]{0:T(1024)S(1)} %bitcast.119), kind=kLoop, calls=%fused_computation.4 | loop fusion | flops 50329600 | bytes 73728 | tf_op jit(solution)/shard_map/reduce_sum | solution.py:45
  100.9 8.4 %select_reduce_fusion.3 = s32[2048]{0:T(1024)S(1)} fusion(s32[8192]{0:T(1024)S(1)} %bitcast.124, s32[8192]{0:T(1024)S(1)} %bitcast.118), kind=kLoop, calls=%fused_computation.6 | loop fusion | flops 50329600 | bytes 73728 | tf_op jit(solution)/shard_map/reduce_sum | solution.py:45
  111.1 8.3 %select_reduce_fusion = s32[2048]{0:T(1024)S(1)} fusion(s32[8192]{0:T(1024)S(1)} %bitcast.123, s32[8192]{0:T(1024)S(1)} %bitcast.117), kind=kLoop, calls=%fused_computation | loop fusion | flops 50329600 | bytes 73728 | tf_op jit(solution)/shard_map/reduce_sum | solution.py:45
  120.2 15.0 %collective-permute-done.11 = bf16[512,2048]{1,0:T(8,128)(2,1)} collective-permute-done((bf16[512,2048]{1,0:T(8,128)(2,1)}, bf16[512,2048]{1,0:T(8,128)(2,1)}, u32[]{:S(2)}, u32[]{:S(2)}) %collective-permute-start.11) | collective-permute-done | bytes 2097184 | tf_op jit(solution)/shard_map/ppermute | solution.py:112
  135.2 11.4 %fusion.28 = bf16[1024,2048]{1,0:T(8,128)(2,1)S(1)} fusion(bf16[512,2048]{1,0:T(8,128)(2,1)} %collective-permute-done.12, bf16[512,2048]{1,0:T(8,128)(2,1)} %collective-permute-done.11, bf16[512,2048]{1,0:T(8,128)(2,1)} %collective-permute-done.10, bf16[512,2048]{1,0:T(8,128)(2,1)} %get-tuple-element.27, s32[2048]{0:T(1024)S(1)} %fusion.141), kind=kOutput, calls=%fused_computation.47 | convolution fusion | flops 8625586176 | bytes 12591104 | tf_op jit(solution)/shard_map/dot_general | solution.py:22
  146.5 19.5 %fusion.63 = bf16[4096,1024]{1,0:T(8,128)(2,1)} fusion(s32[2048]{0:T(1024)S(1)} %bitcast.130, bf16[1024,2048]{1,0:T(8,128)(2,1)S(1)} %fusion.28), kind=kOutput, calls=%fused_computation.80 | convolution fusion | flops 17192452096 | bytes 12591104 | tf_op jit(solution)/shard_map/dot_general | solution.py:22
  166.0 5.1 all-to-all-start.1
  171.2 6.6 %fusion.85 = bf16[2048,512]{1,0:T(8,128)(2,1)S(1)} fusion(bf16[2048,512]{0,1:T(8,128)(2,1)} %all-reduce.4.cloned.1.call-done, s32[2048]{0:T(1024)S(1)} %bitcast.136), kind=kOutput, calls=%fused_computation.106 | convolution fusion | flops 4300210176 | bytes 4202496 | tf_op jit(solution)/shard_map/dot_general | solution.py:22
  181.2 4.8 fusion.84
  187.1 1.5 collective-permute-start.5
  188.6 35.2 %collective-permute-done.1 = bf16[512,2048]{1,0:T(8,128)(2,1)} collective-permute-done((bf16[512,2048]{1,0:T(8,128)(2,1)}, bf16[512,2048]{1,0:T(8,128)(2,1)}, u32[]{:S(2)}, u32[]{:S(2)}) %collective-permute-start.1) | collective-permute-done | bytes 2097184 | tf_op jit(solution)/shard_map/ppermute | solution.py:112
  224.5 1.8 collective-permute-start.7
  226.3 10.9 %fusion.20 = bf16[1024,2048]{1,0:T(8,128)(2,1)S(1)} fusion(bf16[512,2048]{1,0:T(8,128)(2,1)} %collective-permute-done.2, bf16[512,2048]{1,0:T(8,128)(2,1)} %collective-permute-done.1, bf16[512,2048]{1,0:T(8,128)(2,1)} %collective-permute-done, bf16[512,2048]{1,0:T(8,128)(2,1)S(1)} %get-tuple-element.31, s32[2048]{0:T(1024)S(1)} %fusion.139), kind=kOutput, calls=%fused_computation.39 | convolution fusion | flops 8625586176 | bytes 12591104 | tf_op jit(solution)/shard_map/dot_general | solution.py:22
  237.2 19.8 %fusion.62 = bf16[4096,1024]{1,0:T(8,128)(2,1)} fusion(s32[2048]{0:T(1024)S(1)} %bitcast.131, bf16[1024,2048]{1,0:T(8,128)(2,1)S(1)} %fusion.20), kind=kOutput, calls=%fused_computation.79 | convolution fusion | flops 17192452096 | bytes 12591104 | tf_op jit(solution)/shard_map/dot_general | solution.py:22
  257.6 33.0 %all-reduce.7 = bf16[256,256]{1,0:T(8,128)(2,1)S(1)} all-reduce(f32[256,256]{1,0:T(8,128)S(1)} %fusion.112), channel_id=1, replica_groups=mesh['sib'=2,'row'=4,'col'=4] {'sib','row'}, use_global_device_ids=true, to_apply=%region_14.15 | all-reduce | flops 65536 | bytes 393216 | tf_op jit(solution)/shard_map/psum | solution.py:155
  290.7 3.7 fusion.116
  294.4 10.8 %collective-permute-done.8 = bf16[512,512]{1,0:T(8,128)(2,1)S(1)} collective-permute-done((bf16[512,512]{1,0:T(8,128)(2,1)S(1)}, bf16[512,512]{1,0:T(8,128)(2,1)S(1)}, u32[]{:S(2)}, u32[]{:S(2)}) %collective-permute-start.8) | collective-permute-done | bytes 524320 | tf_op jit(solution)/shard_map/ppermute | solution.py:112
  305.2 3.5 fusion.113
  309.9 9.0 %fusion.2 = f32[4096,512]{1,0:T(8,128)S(1)} fusion(s32[2048]{0:T(1024)S(1)} %copy-done.8, bf16[1024,512]{1,0:T(8,128)(2,1)S(1)} %fusion.113, bf16[1024,512]{1,0:T(8,128)(2,1)S(1)} %fusion.116), kind=kOutput, calls=%fused_computation.16 | convolution fusion | flops 8602517504 | bytes 10493952 | tf_op jit(solution)/shard_map/dot_general | solution.py:22
  319.0 9.3 %fusion.64 = f32[4096,512]{1,0:T(8,128)S(1)} fusion(f32[4096,512]{1,0:T(8,128)S(1)} %fusion.2, bf16[2048,512]{1,0:T(8,128)(2,1)S(1)} %collective-permute-done.9, s32[2048]{0:T(1024)S(1)} %copy-done.7), kind=kOutput, calls=%fused_computation.81 | convolution fusion | flops 8600420352 | bytes 18882560 | tf_op jit(solution)/shard_map/dot_general | solution.py:22
  328.4 3.2 copy-done
  332.4 5.0 convolution_convert_fusion
  337.3 3.1 fusion.96
  340.4 4.0 pad_maximum_fusion
  344.4 6.4 %copy.16 = bf16[4096,512]{1,0:T(8,128)(2,1)} copy(bf16[4096,512]{0,1:T(8,128)(2,1)} %pad_maximum_fusion) | data formatting | bytes 8388608
  350.8 3.7 all-to-all-done.1
  354.5 5.2 all-to-all-start
  359.7 4.0 fusion.159
  363.7 10.6 %fusion.76 = bf16[1024,2048]{1,0:T(8,128)(2,1)} fusion(bf16[2048,1024]{1,0:T(8,128)(2,1)S(1)} %bitcast.107, s32[2048]{0:T(1024)S(1)} %copy-done.9), kind=kOutput, calls=%fused_computation.101 | convolution fusion | flops 8596226048 | bytes 8396800 | tf_op jit(solution)/shard_map/dot_general | solution.py:22
  374.3 10.5 %fusion.80 = bf16[1024,2048]{1,0:T(8,128)(2,1)} fusion(bf16[2048,1024]{1,0:T(8,128)(2,1)S(1)} %bitcast.106, s32[2048]{0:T(1024)S(1)} %copy-done.11), kind=kOutput, calls=%fused_computation.103 | convolution fusion | flops 8596226048 | bytes 8396800 | tf_op jit(solution)/shard_map/dot_general | solution.py:22
  384.7 40.5 %fusion.4 = f32[4096,2048]{1,0:T(8,128)} fusion(s32[2048]{0:T(1024)S(1)} %copy-done.12, bf16[1024,2048]{1,0:T(8,128)(2,1)} %fusion.80, bf16[1024,2048]{1,0:T(8,128)(2,1)} %fusion.76), kind=kOutput, calls=%fused_computation.18 | convolution fusion | flops 34384904192 | bytes 41951232 | tf_op jit(solution)/shard_map/dot_general | solution.py:22
  425.2 27.9 %convolution_subtract_fusion = f32[4096,2048]{1,0:T(8,128)} fusion(f32[4096,2048]{1,0:T(8,128)} %fusion.4, bf16[2048,512]{0,1:T(8,128)(2,1)} %all-reduce.6.cloned.1.call-done, bf16[4096,256]{0,1:T(8,128)(2,1)} %convolution_convert_fusion, bf16[4096,256]{0,1:T(8,128)(2,1)S(1)} %convolution_convert_fusion.1), kind=kOutput, calls=%fused_computation.38 | convolution fusion | flops 8606711808 | bytes 73400320 | tf_op jit(solution)/shard_map/dot_general | solution.py:22
  453.1 90.0 %all-to-all-done = bf16[8,512,1024]{2,1,0:T(8,128)(2,1)} async-done(((bf16[8,512,1024]{2,1,0:T(8,128)(2,1)}), bf16[8,512,1024]{2,1,0:T(8,128)(2,1)}, u32[]{:S(2)}, u32[]{:S(2)}) %all-to-all-start) | async-done | bytes 8388640 | tf_op jit(solution)/shard_map/all_to_all | solution.py:121
  543.1 11.0 %fusion.77 = bf16[1024,2048]{1,0:T(8,128)(2,1)S(1)} fusion(s32[2048]{0:T(1024)S(1)} %copy-done.9, bf16[2,2048,1024]{2,1,0:T(8,128)(2,1)} %bitcast.7), kind=kOutput, calls=%fused_computation.102 | convolution fusion | flops 8596226048 | bytes 8396800 | tf_op jit(solution)/shard_map/dot_general | solution.py:22
  554.1 12.6 %fusion.81 = bf16[1024,2048]{1,0:T(8,128)(2,1)} fusion(s32[2048]{0:T(1024)S(1)} %copy-done.11, bf16[2,2048,1024]{2,1,0:T(8,128)(2,1)} %bitcast.7), kind=kOutput, calls=%fused_computation.104 | convolution fusion | flops 8596226048 | bytes 8396800 | tf_op jit(solution)/shard_map/dot_general | solution.py:22
  566.7 41.1 %add_convert_fusion = bf16[4096,2048]{1,0:T(8,128)(2,1)} fusion(f32[4096,2048]{1,0:T(8,128)} %convolution_subtract_fusion, s32[2048]{0:T(1024)S(1)} %copy-done.10, bf16[1024,2048]{1,0:T(8,128)(2,1)} %fusion.81, bf16[1024,2048]{1,0:T(8,128)(2,1)S(1)} %fusion.77), kind=kOutput, calls=%fused_computation.8 | convolution fusion | flops 34401681408 | bytes 58728448 | tf_op jit(solution)/shard_map/dot_general | solution.py:22
  (116 shorter events, 19.3 us)
Async XLA Ops:
  7.2 164.0 %all-reduce.4.cloned.1.call-start = ((), (), s32[]{:S(2)}) async-start(), calls=%async_computation.2 | async-start | bytes 4194304 | tf_op jit(solution)/shard_map/psum | solution.py:152
  14.4 19.7 %copy-start.14 = (s32[1,2048]{1,0:T(1,128)}, s32[1,2048]{1,0:T(1,128)S(1)}, u32[]{:S(2)}) copy-start(s32[1,2048]{1,0:T(1,128)S(1)} %get-tuple-element.22) | copy-start | bytes 24580
  34.1 8.7 %copy-start.16 = (bf16[1,2048,2048]{2,1,0:T(8,128)(2,1)S(1)}, bf16[1,2048,2048]{2,1,0:T(8,128)(2,1)}, u32[]{:S(2)}) copy-start(bf16[1,2048,2048]{2,1,0:T(8,128)(2,1)} %param.3) | copy-start | bytes 25165828
  38.4 81.7 %collective-permute-start.10 = (bf16[512,2048]{1,0:T(8,128)(2,1)}, bf16[512,2048]{1,0:T(8,128)(2,1)}, u32[]{:S(2)}, u32[]{:S(2)}) collective-permute-start(bf16[512,2048]{1,0:T(8,128)(2,1)} %get-tuple-element.30), channel_id=1, source_target_pairs={{0,4},{4,0},{8,12},{12,8},{1,5},{5,1},{9,13},{13,9},{2,6},{6,2},{1... | collective-permute-start | bytes 6291464 | tf_op jit(solution)/shard_map/ppermute | solution.py:112
  41.4 93.8 %collective-permute-start.11 = (bf16[512,2048]{1,0:T(8,128)(2,1)}, bf16[512,2048]{1,0:T(8,128)(2,1)}, u32[]{:S(2)}, u32[]{:S(2)}) collective-permute-start(bf16[512,2048]{1,0:T(8,128)(2,1)} %get-tuple-element.29), channel_id=1, source_target_pairs={{0,8},{4,12},{8,0},{12,4},{1,9},{5,13},{9,1},{13,5},{2,10},{6,14},... | collective-permute-start | bytes 6291464 | tf_op jit(solution)/shard_map/ppermute | solution.py:112
  42.8 92.4 %collective-permute-start.12 = (bf16[512,2048]{1,0:T(8,128)(2,1)}, bf16[512,2048]{1,0:T(8,128)(2,1)}, u32[]{:S(2)}, u32[]{:S(2)}) collective-permute-start(bf16[512,2048]{1,0:T(8,128)(2,1)} %get-tuple-element.28), channel_id=1, source_target_pairs={{0,12},{4,8},{8,4},{12,0},{1,13},{5,9},{9,5},{13,1},{2,14},{6,10},... | collective-permute-start | bytes 6291464 | tf_op jit(solution)/shard_map/ppermute | solution.py:112
  48.6 20.2 %copy-start.5 = (s32[1,2048]{1,0:T(1,128)}, s32[1,2048]{1,0:T(1,128)S(1)}, u32[]{:S(2)}) copy-start(s32[1,2048]{1,0:T(1,128)S(1)} %compare_select_fusion.13) | copy-start | bytes 24580
  71.7 11.9 %copy-start.4 = (s32[2,8192]{1,0:T(2,128)S(1)}, s32[2,8192]{1,0:T(2,128)}, u32[]{:S(2)}) copy-start(s32[2,8192]{1,0:T(2,128)} %param.4) | copy-start | bytes 196612
  71.7 115.5 %collective-permute-start = (bf16[512,2048]{1,0:T(8,128)(2,1)}, bf16[512,2048]{1,0:T(8,128)(2,1)}, u32[]{:S(2)}, u32[]{:S(2)}) collective-permute-start(bf16[512,2048]{1,0:T(8,128)(2,1)} %get-tuple-element.34), channel_id=1, source_target_pairs={{0,4},{4,0},{8,12},{12,8},{1,5},{5,1},{9,13},{13,9},{2,6},{6,2},{1... | collective-permute-start | bytes 6291464 | tf_op jit(solution)/shard_map/ppermute | solution.py:112
  73.7 150.1 %collective-permute-start.1 = (bf16[512,2048]{1,0:T(8,128)(2,1)}, bf16[512,2048]{1,0:T(8,128)(2,1)}, u32[]{:S(2)}, u32[]{:S(2)}) collective-permute-start(bf16[512,2048]{1,0:T(8,128)(2,1)} %get-tuple-element.33), channel_id=1, source_target_pairs={{0,8},{4,12},{8,0},{12,4},{1,9},{5,13},{9,1},{13,5},{2,10},{6,14},... | collective-permute-start | bytes 6291464 | tf_op jit(solution)/shard_map/ppermute | solution.py:112
  120.1 104.4 %collective-permute-start.2 = (bf16[512,2048]{1,0:T(8,128)(2,1)}, bf16[512,2048]{1,0:T(8,128)(2,1)}, u32[]{:S(2)}, u32[]{:S(2)}) collective-permute-start(bf16[512,2048]{1,0:T(8,128)(2,1)} %get-tuple-element.32), channel_id=1, source_target_pairs={{0,12},{4,8},{8,4},{12,0},{1,13},{5,9},{9,5},{13,1},{2,14},{6,10},... | collective-permute-start | bytes 6291464 | tf_op jit(solution)/shard_map/ppermute | solution.py:112
  166.0 5.2 copy-start.15
  166.0 188.5 %all-to-all-start.1 = ((bf16[8,512,1024]{2,1,0:T(8,128)(2,1)}), bf16[8,512,1024]{2,1,0:T(8,128)(2,1)}, u32[]{:S(2)}, u32[]{:S(2)}) async-start(bf16[8,512,1024]{2,1,0:T(8,128)(2,1)} %bitcast.104), calls=%async_computation.1 | async-start | bytes 16777216 | tf_op jit(solution)/shard_map/all_to_all | solution.py:121
  171.1 254.1 %all-reduce.6.cloned.1.call-start = ((), (), s32[]{:S(2)}) async-start(), calls=%async_computation.3 | async-start | bytes 4194304 | tf_op jit(solution)/shard_map/psum | solution.py:13
  177.8 3.4 copy-start.6
  177.8 3.4 copy-start.17
  179.1 111.4 %collective-permute-start.3 = (bf16[512,512]{1,0:T(8,128)(2,1)}, bf16[512,512]{1,0:T(8,128)(2,1)}, u32[]{:S(2)}, u32[]{:S(2)}) collective-permute-start(bf16[512,512]{1,0:T(8,128)(2,1)} %get-tuple-element.38), channel_id=1, source_target_pairs={{0,4},{4,0},{8,12},{12,8},{1,5},{5,1},{9,13},{13,9},{2,6},{6,2},{1... | collective-permute-start | bytes 1572872 | tf_op jit(solution)/shard_map/ppermute | solution.py:112
  180.0 110.6 %collective-permute-start.4 = (bf16[512,512]{1,0:T(8,128)(2,1)}, bf16[512,512]{1,0:T(8,128)(2,1)}, u32[]{:S(2)}, u32[]{:S(2)}) collective-permute-start(bf16[512,512]{1,0:T(8,128)(2,1)} %get-tuple-element.37), channel_id=1, source_target_pairs={{0,8},{4,12},{8,0},{12,4},{1,9},{5,13},{9,1},{13,5},{2,10},{6,14},... | collective-permute-start | bytes 1572872 | tf_op jit(solution)/shard_map/ppermute | solution.py:112
  187.1 103.5 %collective-permute-start.5 = (bf16[512,512]{1,0:T(8,128)(2,1)}, bf16[512,512]{1,0:T(8,128)(2,1)}, u32[]{:S(2)}, u32[]{:S(2)}) collective-permute-start(bf16[512,512]{1,0:T(8,128)(2,1)} %get-tuple-element.36), channel_id=1, source_target_pairs={{0,12},{4,8},{8,4},{12,0},{1,13},{5,9},{9,5},{13,1},{2,14},{6,10},... | collective-permute-start | bytes 1572872 | tf_op jit(solution)/shard_map/ppermute | solution.py:112
  223.8 70.6 %collective-permute-start.6 = (bf16[512,512]{1,0:T(8,128)(2,1)}, bf16[512,512]{1,0:T(8,128)(2,1)}, u32[]{:S(2)}, u32[]{:S(2)}) collective-permute-start(bf16[512,512]{1,0:T(8,128)(2,1)} %get-tuple-element.42), channel_id=1, source_target_pairs={{0,4},{4,0},{8,12},{12,8},{1,5},{5,1},{9,13},{13,9},{2,6},{6,2},{1... | collective-permute-start | bytes 1572872 | tf_op jit(solution)/shard_map/ppermute | solution.py:112
  224.5 69.9 %collective-permute-start.7 = (bf16[512,512]{1,0:T(8,128)(2,1)}, bf16[512,512]{1,0:T(8,128)(2,1)}, u32[]{:S(2)}, u32[]{:S(2)}) collective-permute-start(bf16[512,512]{1,0:T(8,128)(2,1)} %get-tuple-element.41), channel_id=1, source_target_pairs={{0,8},{4,12},{8,0},{12,4},{1,9},{5,13},{9,1},{13,5},{2,10},{6,14},... | collective-permute-start | bytes 1572872 | tf_op jit(solution)/shard_map/ppermute | solution.py:112
  237.2 19.9 %copy-start.13 = (s32[1,2048]{1,0:T(1,128)S(1)}, s32[1,2048]{1,0:T(1,128)}, u32[]{:S(2)}) copy-start(s32[1,2048]{1,0:T(1,128)} %get-tuple-element.74) | copy-start | bytes 24580
  237.2 53.4 %copy-start.3 = (bf16[512,512]{1,0:T(8,128)(2,1)S(1)}, bf16[512,512]{1,0:T(8,128)(2,1)}, u32[]{:S(2)}) copy-start(bf16[512,512]{1,0:T(8,128)(2,1)} %get-tuple-element.40) | copy-start | bytes 1572868
  237.2 53.5 %copy-start.2 = (bf16[512,512]{1,0:T(8,128)(2,1)S(1)}, bf16[512,512]{1,0:T(8,128)(2,1)}, u32[]{:S(2)}) copy-start(bf16[512,512]{1,0:T(8,128)(2,1)} %get-tuple-element.35) | copy-start | bytes 1572868
  290.6 14.6 %collective-permute-start.8 = (bf16[512,512]{1,0:T(8,128)(2,1)S(1)}, bf16[512,512]{1,0:T(8,128)(2,1)S(1)}, u32[]{:S(2)}, u32[]{:S(2)}) collective-permute-start(bf16[512,512]{1,0:T(8,128)(2,1)S(1)} %copy-done.3), channel_id=1, source_target_pairs={{0,12},{4,8},{8,4},{12,0},{1,13},{5,9},{9,5},{13,1},{2,14},{6,10},... | collective-permute-start | bytes 1572872 | tf_op jit(solution)/shard_map/ppermute | solution.py:112
  308.7 1.0 copy-start.1
  308.8 1.2 copy-start.8
  308.9 10.1 %collective-permute-start.9 = (bf16[2048,512]{1,0:T(8,128)(2,1)S(1)}, bf16[2048,512]{1,0:T(8,128)(2,1)S(1)}, u32[]{:S(2)}, u32[]{:S(2)}) collective-permute-start(bf16[2048,512]{1,0:T(8,128)(2,1)S(1)} %pad_maximum_fusion.1), channel_id=1, source_target_pairs={{0,16},{16,0},{1,17},{17,1},{2,18},{18,2},{3,19},{19,3},{4,20},{20... | collective-permute-start | bytes 6291464 | tf_op jit(solution)/shard_map/ppermute | solution.py:161
  309.9 9.1 %copy-start.7 = (s32[2048]{0:T(1024)S(1)}, s32[2048]{0:T(1024)}, u32[]{:S(2)}) copy-start(s32[2048]{0:T(1024)} %get-tuple-element.59) | copy-start | bytes 24580
  328.4 3.2 copy-start
  354.5 188.6 %all-to-all-start = ((bf16[8,512,1024]{2,1,0:T(8,128)(2,1)}), bf16[8,512,1024]{2,1,0:T(8,128)(2,1)}, u32[]{:S(2)}, u32[]{:S(2)}) async-start(bf16[8,512,1024]{2,1,0:T(8,128)(2,1)} %bitcast.105), calls=%async_computation | async-start | bytes 16777216 | tf_op jit(solution)/shard_map/all_to_all | solution.py:121
  359.7 4.0 copy-start.9
  363.7 10.6 %copy-start.11 = (s32[2048]{0:T(1024)S(1)}, s32[2048]{0:T(1024)}, u32[]{:S(2)}) copy-start(s32[2048]{0:T(1024)} %broadcast_add_fusion.5) | copy-start | bytes 24580
  374.3 10.5 %copy-start.12 = (s32[2048]{0:T(1024)S(1)}, s32[2048]{0:T(1024)}, u32[]{:S(2)}) copy-start(s32[2048]{0:T(1024)} %pad_add_fusion) | copy-start | bytes 24580
  554.1 12.6 %copy-start.10 = (s32[2048]{0:T(1024)S(1)}, s32[2048]{0:T(1024)}, u32[]{:S(2)}) copy-start(s32[2048]{0:T(1024)} %pad_add_fusion.1) | copy-start | bytes 24580
Sparse Core Ops, SparseCore 0:
  48.7 88.3 all-reduce.3
  340.5 69.1 all-reduce.5

commit v4 on v3

--- a/solution.py
+++ b/solution.py
@@ -13,7 +13,7 @@
     return lax.psum(jnp.where(mine, shard, jnp.zeros_like(shard)), axis)
 
 
-CHUNKS = 2
+CHUNKS = 4
 LAST = (((1,), (1,)), ((), ()))
 PLAIN = (((1,), (0,)), ((), ()))
 
@@ -197,8 +197,8 @@
     front_block = placed(0)
     across, front_block = lax.optimization_barrier((across, front_block))
     front_block = front_block - dot(factor, across, LAST)
-    landed[1:], front_block = lax.optimization_barrier((landed[1:], front_block))
     for part in range(1, CHUNKS):
+        landed[part], front_block = lax.optimization_barrier((landed[part], front_block))
         front_block = front_block + placed(part)
     return front_block.astype(jnp.bfloat16), factor
 

time: 623 us -> 701 us (1.13)
  matrix products: 305 us -> 344 us
  starting transfers between devices: 23.7 us -> 46.7 us
  waiting for transfers between devices: 156 us -> 166 us
    dot_general x24 -> x40, matrix products: 305 us -> 344 us  [dot(): return lax.dot_general(a, b, dims, preferred_element_type=jnp.float32)]
    ppermute x12 -> x24, waiting for transfers between devices: 61.8 us -> 82.3 us  [exchange(): blocks.append(lax.ppermute(block, 'row', pairs))]
    ppermute x12 -> x24, starting transfers between devices: 13.3 us -> 27.2 us  [exchange(): blocks.append(lax.ppermute(block, 'row', pairs))]
    all_to_all x2 -> x4, waiting for transfers between devices: 93.7 us -> 84.2 us  [on_device(): lax.all_to_all(send_cols.reshape(groups, cap_cols, held_count), ('sib', '...]
    all_to_all x2 -> x4, starting transfers between devices: 10.3 us -> 19.3 us  [on_device(): lax.all_to_all(send_cols.reshape(groups, cap_cols, held_count), ('sib', '...]
  transfers between devices with their start and end apart: 17 -> 31, of which waited for: 6 -> 17; matrix products, arithmetic and copies ran while one was open for 47% -> 53% of each run, Pallas kernels for 0% -> 0%
where the time goes in v4:
time: 701 us; the launch traced here: 692 us
  matrix products  344 us (49%)
  waiting for transfers between devices  166 us (24%)
  other arithmetic  62.1 us (9%)
  starting transfers between devices  46.7 us (7%)
  blocking collectives  32.2 us (5%)
  local copies, waits for them, and re-layouts  25.6 us (4%)
  between operations  15.1 us (2%)
    dot_general x40, matrix products, dot(): return lax.dot_general(a, b, dims, preferred_element_type=jnp.float32)  344 us
    all_to_all x4, waiting for transfers between devices, on_device(): lax.all_to_all(send_cols.reshape(groups, cap_cols, held_count), ('sib', '...  84.2 us
    ppermute x24, waiting for transfers between devices, exchange(): blocks.append(lax.ppermute(block, 'row', pairs))  82.3 us
    reduce_sum x4, other arithmetic, at_place(): return jnp.sum(jnp.where(here, value[None, :] + 1, 0), axis=1) - 1  33.3 us
    psum x1, blocking collectives, on_device(): tops = lax.psum(tops, ('sib', 'row'))  32.2 us
    ppermute x24, starting transfers between devices, exchange(): blocks.append(lax.ppermute(block, 'row', pairs))  27.2 us
    all_to_all x4, starting transfers between devices, on_device(): lax.all_to_all(send_cols.reshape(groups, cap_cols, held_count), ('sib', '...  19.3 us
  transfers between devices with their start and end apart: 31, of which 17 were waited for; matrix products, arithmetic and copies ran while one was open for 53% of the time, Pallas kernels for 0%

profile of v4, /device:TPU:0, one launch (start us, length us, event | category | flops | bytes accessed | tf_op | source)
XLA Modules:
  0.0 692.5 jit_solution(8213807215505692805)
XLA Ops:
  14.4 11.2 %fusion.114 = bf16[1024,2048]{1,0:T(8,128)(2,1)S(1)} fusion(bf16[1,2048,2048]{2,1,0:T(8,128)(2,1)} %param.3, s32[2048]{0:T(1024)S(1)} %bitcast.169), kind=kOutput, calls=%fused_computation.141 | convolution fusion | flops 8594128896 | bytes 12591104 | tf_op jit(solution)/shard_map/dot_general | solution.py:22
  31.9 9.1 %fusion.140 = bf16[2048,512]{0,1:T(8,128)(2,1)} fusion(bf16[1,2048,2048]{2,1,0:T(8,128)(2,1)} %param.3, s32[2048]{0:T(1024)S(1)} %bitcast.171), kind=kOutput, calls=%fused_computation.155 | convolution fusion | flops 4297064448 | bytes 10493952 | tf_op jit(solution)/shard_map/dot_general | solution.py:22
  41.7 11.7 %fusion.111 = bf16[1024,2048]{1,0:T(8,128)(2,1)S(1)} fusion(bf16[1,2048,2048]{2,1,0:T(8,128)(2,1)} %param.3, s32[2048]{0:T(1024)S(1)} %bitcast.162), kind=kOutput, calls=%fused_computation.140 | convolution fusion | flops 8594128896 | bytes 12591104 | tf_op jit(solution)/shard_map/dot_general | solution.py:22
  59.9 4.8 reduce-window.14
  70.3 8.4 %select_reduce_fusion.1 = s32[2048]{0:T(1024)S(1)} fusion(s32[8192]{0:T(1024)S(1)} %bitcast.152, s32[8192]{0:T(1024)S(1)} %bitcast.148), kind=kLoop, calls=%fused_computation.2 | loop fusion | flops 50329600 | bytes 73728 | tf_op jit(solution)/shard_map/reduce_sum | solution.py:45
  79.2 8.3 %select_reduce_fusion = s32[2048]{0:T(1024)S(1)} fusion(s32[8192]{0:T(1024)S(1)} %bitcast.151, s32[8192]{0:T(1024)S(1)} %bitcast.147), kind=kLoop, calls=%fused_computation | loop fusion | flops 50329600 | bytes 73728 | tf_op jit(solution)/shard_map/reduce_sum | solution.py:45
  88.1 8.3 %select_reduce_fusion.2 = s32[2048]{0:T(1024)S(1)} fusion(s32[8192]{0:T(1024)S(1)} %bitcast.150, s32[8192]{0:T(1024)S(1)} %bitcast.146), kind=kLoop, calls=%fused_computation.4 | loop fusion | flops 50329600 | bytes 73728 | tf_op jit(solution)/shard_map/reduce_sum | solution.py:45
  96.4 8.4 %select_reduce_fusion.3 = s32[2048]{0:T(1024)S(1)} fusion(s32[8192]{0:T(1024)S(1)} %bitcast.149, s32[8192]{0:T(1024)S(1)} %bitcast.145), kind=kLoop, calls=%fused_computation.6 | loop fusion | flops 50329600 | bytes 73728 | tf_op jit(solution)/shard_map/reduce_sum | solution.py:45
  105.5 12.7 %fusion.108 = bf16[1024,2048]{1,0:T(8,128)(2,1)} fusion(bf16[1,2048,2048]{2,1,0:T(8,128)(2,1)} %param.3, s32[2048]{0:T(1024)} %bitcast.160), kind=kOutput, calls=%fused_computation.139 | convolution fusion | flops 8594128896 | bytes 12591104 | tf_op jit(solution)/shard_map/dot_general | solution.py:22
  118.2 12.5 %fusion.105 = bf16[1024,2048]{1,0:T(8,128)(2,1)} fusion(bf16[1,2048,2048]{2,1,0:T(8,128)(2,1)} %param.3, s32[2048]{0:T(1024)S(1)} %bitcast.158), kind=kOutput, calls=%fused_computation.138 | convolution fusion | flops 8594128896 | bytes 12591104 | tf_op jit(solution)/shard_map/dot_general | solution.py:22
  133.2 4.5 fusion.283
  143.4 4.2 fusion.117.clone.2
  147.6 10.9 %fusion.51 = bf16[4096,512]{1,0:T(8,128)(2,1)} fusion(s32[2048]{0:T(1024)S(1)} %bitcast.164, bf16[512,2048]{1,0:T(8,128)(2,1)S(1)} %fusion.117.clone.2), kind=kOutput, calls=%fused_computation.76 | convolution fusion | flops 8600420352 | bytes 6299648 | tf_op jit(solution)/shard_map/dot_general | solution.py:22
  158.5 5.0 all-to-all-start.3
  167.6 4.2 fusion.120.clone.2
  171.8 10.6 %fusion.50 = bf16[4096,512]{1,0:T(8,128)(2,1)} fusion(s32[2048]{0:T(1024)S(1)} %bitcast.165, bf16[512,2048]{1,0:T(8,128)(2,1)S(1)} %fusion.120.clone.2), kind=kOutput, calls=%fused_computation.75 | convolution fusion | flops 8600420352 | bytes 6299648 | tf_op jit(solution)/shard_map/dot_general | solution.py:22
  182.4 6.2 collective-permute-done.3
  190.0 21.9 %collective-permute-done.5 = bf16[256,2048]{1,0:T(8,128)(2,1)S(1)} collective-permute-done((bf16[256,2048]{1,0:T(8,128)(2,1)}, bf16[256,2048]{1,0:T(8,128)(2,1)S(1)}, u32[]{:S(2)}, u32[]{:S(2)}) %collective-permute-start.5) | collective-permute-done | bytes 1048608 | tf_op jit(solution)/shard_map/ppermute | solution.py:112
  215.8 10.5 %fusion.49 = bf16[4096,512]{1,0:T(8,128)(2,1)} fusion(s32[2048]{0:T(1024)S(1)} %bitcast.166, bf16[512,2048]{1,0:T(8,128)(2,1)S(1)} %fusion.123.clone.2), kind=kOutput, calls=%fused_computation.74 | convolution fusion | flops 8600420352 | bytes 6299648 | tf_op jit(solution)/shard_map/dot_general | solution.py:22
  226.4 7.1 %collective-permute-done = bf16[256,2048]{1,0:T(8,128)(2,1)S(1)} collective-permute-done((bf16[256,2048]{1,0:T(8,128)(2,1)}, bf16[256,2048]{1,0:T(8,128)(2,1)S(1)}, u32[]{:S(2)}, u32[]{:S(2)}) %collective-permute-start) | collective-permute-done | bytes 1048608 | tf_op jit(solution)/shard_map/ppermute | solution.py:112
  234.2 20.1 %collective-permute-done.2 = bf16[256,2048]{1,0:T(8,128)(2,1)S(1)} collective-permute-done((bf16[256,2048]{1,0:T(8,128)(2,1)S(1)}, bf16[256,2048]{1,0:T(8,128)(2,1)S(1)}, u32[]{:S(2)}, u32[]{:S(2)}) %collective-permute-start.2) | collective-permute-done | bytes 1048608 | tf_op jit(solution)/shard_map/ppermute | solution.py:112
  257.0 10.5 %fusion.48 = bf16[4096,512]{1,0:T(8,128)(2,1)} fusion(s32[2048]{0:T(1024)S(1)} %bitcast.167, bf16[512,2048]{1,0:T(8,128)(2,1)S(1)} %fusion.126.clone.5), kind=kOutput, calls=%fused_computation.73 | convolution fusion | flops 8600420352 | bytes 6299648 | tf_op jit(solution)/shard_map/dot_general | solution.py:22
  288.7 5.0 collective-permute-done.12
  306.5 4.3 collective-permute-done.17
  320.3 32.2 %all-reduce.7 = bf16[256,256]{1,0:T(8,128)(2,1)S(1)} all-reduce(f32[256,256]{1,0:T(8,128)S(1)} %fusion.173), channel_id=1, replica_groups=mesh['sib'=2,'row'=4,'col'=4] {'sib','row'}, use_global_device_ids=true, to_apply=%region_14.15 | all-reduce | flops 65536 | bytes 393216 | tf_op jit(solution)/shard_map/psum | solution.py:155
  352.8 4.8 all-to-all-start.2
  357.6 10.4 %fusion.4 = f32[4096,512]{1,0:T(8,128)S(1)} fusion(s32[2048]{0:T(1024)S(1)} %copy-done.16, bf16[512,512]{1,0:T(8,128)(2,1)} %copy-done.10, bf16[512,512]{1,0:T(8,128)(2,1)} %copy-done.9, bf16[512,512]{1,0:T(8,128)(2,1)} %copy-done.8, bf16[512,512]{1,0:T(8,128)(2,1)S(1)} %fusion.181), kind=kOutput, calls=%fused_computation.16 | convolution fusion | flops 8606711808 | bytes 10493952 | tf_op jit(solution)/shard_map/dot_general | solution.py:22
  368.1 10.9 %fusion.47 = f32[4096,512]{1,0:T(8,128)S(1)} fusion(f32[4096,512]{1,0:T(8,128)S(1)} %fusion.4, bf16[2048,512]{1,0:T(8,128)(2,1)} %collective-permute-done.21, s32[2048]{0:T(1024)S(1)} %copy-done.15), kind=kOutput, calls=%fused_computation.72 | convolution fusion | flops 8600420352 | bytes 18882560 | tf_op jit(solution)/shard_map/dot_general | solution.py:22
  383.2 4.9 convolution_convert_fusion
  395.2 6.4 copy.16
  404.2 6.1 fusion.129
  410.3 6.0 fusion.133
  416.3 34.9 %all-to-all-done.2 = bf16[8,512,512]{2,1,0:T(8,128)(2,1)} async-done(((bf16[8,512,512]{2,1,0:T(8,128)(2,1)}), bf16[8,512,512]{2,1,0:T(8,128)(2,1)}, u32[]{:S(2)}, u32[]{:S(2)}) %all-to-all-start.2) | async-done | bytes 4194336 | tf_op jit(solution)/shard_map/all_to_all | solution.py:121
  451.2 4.9 all-to-all-start.1
  456.1 22.6 %fusion.20 = f32[4096,2048]{1,0:T(8,128)} fusion(s32[1024]{0:T(1024)S(1)} %copy-done.25, bf16[512,2048]{1,0:T(8,128)(2,1)} %fusion.133, bf16[512,2048]{1,0:T(8,128)(2,1)} %fusion.129), kind=kOutput, calls=%fused_computation.40 | convolution fusion | flops 17192452096 | bytes 37752832 | tf_op jit(solution)/shard_map/dot_general | solution.py:22
  478.7 27.5 %convolution_subtract_fusion = f32[4096,2048]{1,0:T(8,128)} fusion(f32[4096,2048]{1,0:T(8,128)} %fusion.20, bf16[2048,512]{0,1:T(8,128)(2,1)} %all-reduce.6.cloned.1.call-done, bf16[4096,256]{0,1:T(8,128)(2,1)} %convolution_convert_fusion, bf16[4096,256]{0,1:T(8,128)(2,1)S(1)} %convolution_convert_fusion.1), kind=kOutput, calls=%fused_computation.41 | convolution fusion | flops 8606711808 | bytes 73400320 | tf_op jit(solution)/shard_map/dot_general | solution.py:22
  506.1 7.6 %fusion.130 = bf16[512,2048]{1,0:T(8,128)(2,1)} fusion(s32[2048]{0:T(1024)S(1)} %copy-done.17, bf16[2,2048,512]{2,1,0:T(8,128)(2,1)} %bitcast.13), kind=kOutput, calls=%fused_computation.147 | convolution fusion | flops 4300210176 | bytes 4202496 | tf_op jit(solution)/shard_map/dot_general | solution.py:22
  513.7 7.9 %fusion.134 = bf16[512,2048]{1,0:T(8,128)(2,1)} fusion(s32[2048]{0:T(1024)S(1)} %copy-done.18, bf16[2,2048,512]{2,1,0:T(8,128)(2,1)} %bitcast.13), kind=kOutput, calls=%fused_computation.151 | convolution fusion | flops 4300210176 | bytes 4202496 | tf_op jit(solution)/shard_map/dot_general | solution.py:22
  521.7 27.9 %all-to-all-done.1 = bf16[8,512,512]{2,1,0:T(8,128)(2,1)} async-done(((bf16[8,512,512]{2,1,0:T(8,128)(2,1)}), bf16[8,512,512]{2,1,0:T(8,128)(2,1)}, u32[]{:S(2)}, u32[]{:S(2)}) %all-to-all-start.1) | async-done | bytes 4194336 | tf_op jit(solution)/shard_map/all_to_all | solution.py:121
  549.6 4.7 all-to-all-start
  554.3 30.0 %convolution_add_fusion.1 = f32[4096,2048]{1,0:T(8,128)} fusion(f32[4096,2048]{1,0:T(8,128)} %convolution_subtract_fusion, s32[1024]{0:T(1024)S(1)} %copy-done.24, bf16[512,2048]{1,0:T(8,128)(2,1)} %fusion.134, bf16[512,2048]{1,0:T(8,128)(2,1)} %fusion.130), kind=kOutput, calls=%fused_computation.19 | convolution fusion | flops 17200840704 | bytes 71307264 | tf_op jit(solution)/shard_map/dot_general | solution.py:22
  584.3 6.6 fusion.131
  590.9 6.6 fusion.135
  597.5 29.0 %convolution_add_fusion = f32[4096,2048]{1,0:T(8,128)} fusion(f32[4096,2048]{1,0:T(8,128)} %convolution_add_fusion.1, s32[1024]{0:T(1024)S(1)} %copy-done.23, bf16[512,2048]{1,0:T(8,128)(2,1)S(1)} %fusion.135, bf16[512,2048]{1,0:T(8,128)(2,1)S(1)} %fusion.131), kind=kOutput, calls=%fused_computation.18 | convolution fusion | flops 17200840704 | bytes 71307264 | tf_op jit(solution)/shard_map/dot_general | solution.py:22
  626.5 21.3 %all-to-all-done = bf16[8,512,512]{2,1,0:T(8,128)(2,1)} async-done(((bf16[8,512,512]{2,1,0:T(8,128)(2,1)}), bf16[8,512,512]{2,1,0:T(8,128)(2,1)}, u32[]{:S(2)}, u32[]{:S(2)}) %all-to-all-start) | async-done | bytes 4194336 | tf_op jit(solution)/shard_map/all_to_all | solution.py:121
  647.8 6.6 fusion.132
  654.4 6.6 fusion.136
  661.0 24.4 %add_convert_fusion = bf16[4096,2048]{1,0:T(8,128)(2,1)} fusion(f32[4096,2048]{1,0:T(8,128)} %convolution_add_fusion, s32[1024]{0:T(1024)S(1)} %copy-done.22, bf16[512,2048]{1,0:T(8,128)(2,1)S(1)} %fusion.136, bf16[512,2048]{1,0:T(8,128)(2,1)S(1)} %fusion.132), kind=kOutput, calls=%fused_computation.8 | convolution fusion | flops 17209229312 | bytes 54530048 | tf_op jit(solution)/shard_map/dot_general | solution.py:22
  (190 shorter events, 106.3 us)
Async XLA Ops:
  7.2 260.4 %all-reduce.4.cloned.1.call-start = ((), (), s32[]{:S(2)}) async-start(), calls=%async_computation.4 | async-start | bytes 4194304 | tf_op jit(solution)/shard_map/psum | solution.py:152
  14.4 11.2 %copy-start.20 = (s32[1,2048]{1,0:T(1,128)}, s32[1,2048]{1,0:T(1,128)S(1)}, u32[]{:S(2)}) copy-start(s32[1,2048]{1,0:T(1,128)S(1)} %get-tuple-element.30) | copy-start | bytes 24580
  27.5 112.4 %collective-permute-start.22 = (bf16[256,2048]{1,0:T(8,128)(2,1)}, bf16[256,2048]{1,0:T(8,128)(2,1)}, u32[]{:S(2)}, u32[]{:S(2)}) collective-permute-start(bf16[256,2048]{1,0:T(8,128)(2,1)} %get-tuple-element.38), channel_id=1, source_target_pairs={{0,4},{4,0},{8,12},{12,8},{1,5},{5,1},{9,13},{13,9},{2,6},{6,2},{1... | collective-permute-start | bytes 3145736 | tf_op jit(solution)/shard_map/ppermute | solution.py:112
  30.4 109.5 %collective-permute-start.23 = (bf16[256,2048]{1,0:T(8,128)(2,1)}, bf16[256,2048]{1,0:T(8,128)(2,1)}, u32[]{:S(2)}, u32[]{:S(2)}) collective-permute-start(bf16[256,2048]{1,0:T(8,128)(2,1)} %get-tuple-element.37), channel_id=1, source_target_pairs={{0,8},{4,12},{8,0},{12,4},{1,9},{5,13},{9,1},{13,5},{2,10},{6,14},... | collective-permute-start | bytes 3145736 | tf_op jit(solution)/shard_map/ppermute | solution.py:112
  31.9 110.0 %collective-permute-start.24 = (bf16[256,2048]{1,0:T(8,128)(2,1)}, bf16[256,2048]{1,0:T(8,128)(2,1)}, u32[]{:S(2)}, u32[]{:S(2)}) collective-permute-start(bf16[256,2048]{1,0:T(8,128)(2,1)} %get-tuple-element.36), channel_id=1, source_target_pairs={{0,12},{4,8},{8,4},{12,0},{1,13},{5,9},{9,5},{13,1},{2,14},{6,10},... | collective-permute-start | bytes 3145736 | tf_op jit(solution)/shard_map/ppermute | solution.py:112
  41.7 11.7 %copy-start.13 = (s32[1,2048]{1,0:T(1,128)}, s32[1,2048]{1,0:T(1,128)S(1)}, u32[]{:S(2)}) copy-start(s32[1,2048]{1,0:T(1,128)S(1)} %get-tuple-element.85) | copy-start | bytes 24580
  55.1 15.0 %copy-start.11 = (s32[2,8192]{1,0:T(2,128)S(1)}, s32[2,8192]{1,0:T(2,128)}, u32[]{:S(2)}) copy-start(s32[2,8192]{1,0:T(2,128)} %param.4) | copy-start | bytes 196612
  55.1 108.3 %collective-permute-start.6 = (bf16[256,2048]{1,0:T(8,128)(2,1)}, bf16[256,2048]{1,0:T(8,128)(2,1)}, u32[]{:S(2)}, u32[]{:S(2)}) collective-permute-start(bf16[256,2048]{1,0:T(8,128)(2,1)} %get-tuple-element.42), channel_id=1, source_target_pairs={{0,4},{4,0},{8,12},{12,8},{1,5},{5,1},{9,13},{13,9},{2,6},{6,2},{1... | collective-permute-start | bytes 3145736 | tf_op jit(solution)/shard_map/ppermute | solution.py:112
  57.2 106.8 %collective-permute-start.7 = (bf16[256,2048]{1,0:T(8,128)(2,1)}, bf16[256,2048]{1,0:T(8,128)(2,1)}, u32[]{:S(2)}, u32[]{:S(2)}) collective-permute-start(bf16[256,2048]{1,0:T(8,128)(2,1)} %get-tuple-element.41), channel_id=1, source_target_pairs={{0,8},{4,12},{8,0},{12,4},{1,9},{5,13},{9,1},{13,5},{2,10},{6,14},... | collective-permute-start | bytes 3145736 | tf_op jit(solution)/shard_map/ppermute | solution.py:112
  139.9 27.1 %collective-permute-start.8 = (bf16[256,2048]{1,0:T(8,128)(2,1)S(1)}, bf16[256,2048]{1,0:T(8,128)(2,1)}, u32[]{:S(2)}, u32[]{:S(2)}) collective-permute-start(bf16[256,2048]{1,0:T(8,128)(2,1)S(1)} %copy-done.2), channel_id=1, source_target_pairs={{0,12},{4,8},{8,4},{12,0},{1,13},{5,9},{9,5},{13,1},{2,14},{6,10},... | collective-permute-start | bytes 3145736 | tf_op jit(solution)/shard_map/ppermute | solution.py:112
  139.9 48.7 %collective-permute-start.3 = (bf16[256,2048]{1,0:T(8,128)(2,1)}, bf16[256,2048]{1,0:T(8,128)(2,1)}, u32[]{:S(2)}, u32[]{:S(2)}) collective-permute-start(bf16[256,2048]{1,0:T(8,128)(2,1)} %get-tuple-element.46), channel_id=1, source_target_pairs={{0,4},{4,0},{8,12},{12,8},{1,5},{5,1},{9,13},{13,9},{2,6},{6,2},{1... | collective-permute-start | bytes 3145736 | tf_op jit(solution)/shard_map/ppermute | solution.py:112
  141.9 48.1 %collective-permute-start.4 = (bf16[256,2048]{1,0:T(8,128)(2,1)}, bf16[256,2048]{1,0:T(8,128)(2,1)}, u32[]{:S(2)}, u32[]{:S(2)}) collective-permute-start(bf16[256,2048]{1,0:T(8,128)(2,1)} %get-tuple-element.45), channel_id=1, source_target_pairs={{0,8},{4,12},{8,0},{12,4},{1,9},{5,13},{9,1},{13,5},{2,10},{6,14},... | collective-permute-start | bytes 3145736 | tf_op jit(solution)/shard_map/ppermute | solution.py:112
  158.5 8.6 %copy-start.5 = (bf16[256,2048]{1,0:T(8,128)(2,1)S(1)}, bf16[256,2048]{1,0:T(8,128)(2,1)}, u32[]{:S(2)}) copy-start(bf16[256,2048]{1,0:T(8,128)(2,1)} %get-tuple-element.49) | copy-start | bytes 3145732
  158.5 194.3 %all-to-all-start.3 = ((bf16[8,512,512]{2,1,0:T(8,128)(2,1)}), bf16[8,512,512]{2,1,0:T(8,128)(2,1)}, u32[]{:S(2)}, u32[]{:S(2)}) async-start(bf16[8,512,512]{2,1,0:T(8,128)(2,1)} %bitcast.133), calls=%async_computation.3 | async-start | bytes 8388608 | tf_op jit(solution)/shard_map/all_to_all | solution.py:121
  163.5 48.4 %collective-permute-start.5 = (bf16[256,2048]{1,0:T(8,128)(2,1)}, bf16[256,2048]{1,0:T(8,128)(2,1)S(1)}, u32[]{:S(2)}, u32[]{:S(2)}) collective-permute-start(bf16[256,2048]{1,0:T(8,128)(2,1)} %get-tuple-element.44), channel_id=1, source_target_pairs={{0,12},{4,8},{8,4},{12,0},{1,13},{5,9},{9,5},{13,1},{2,14},{6,10},... | collective-permute-start | bytes 3145736 | tf_op jit(solution)/shard_map/ppermute | solution.py:112
  164.0 69.5 %collective-permute-start = (bf16[256,2048]{1,0:T(8,128)(2,1)}, bf16[256,2048]{1,0:T(8,128)(2,1)S(1)}, u32[]{:S(2)}, u32[]{:S(2)}) collective-permute-start(bf16[256,2048]{1,0:T(8,128)(2,1)} %get-tuple-element.50), channel_id=1, source_target_pairs={{0,4},{4,0},{8,12},{12,8},{1,5},{5,1},{9,13},{13,9},{2,6},{6,2},{1... | collective-permute-start | bytes 3145736 | tf_op jit(solution)/shard_map/ppermute | solution.py:112
  167.0 67.2 %collective-permute-start.1 = (bf16[256,2048]{1,0:T(8,128)(2,1)S(1)}, bf16[256,2048]{1,0:T(8,128)(2,1)S(1)}, u32[]{:S(2)}, u32[]{:S(2)}) collective-permute-start(bf16[256,2048]{1,0:T(8,128)(2,1)S(1)} %copy-done.5), channel_id=1, source_target_pairs={{0,8},{4,12},{8,0},{12,4},{1,9},{5,13},{9,1},{13,5},{2,10},{6,14},... | collective-permute-start | bytes 3145736 | tf_op jit(solution)/shard_map/ppermute | solution.py:112
  171.8 16.8 %copy-start.4 = (bf16[256,2048]{1,0:T(8,128)(2,1)S(1)}, bf16[256,2048]{1,0:T(8,128)(2,1)}, u32[]{:S(2)}) copy-start(bf16[256,2048]{1,0:T(8,128)(2,1)} %get-tuple-element.48) | copy-start | bytes 3145732
  171.8 40.1 %copy-start.6 = (bf16[256,2048]{1,0:T(8,128)(2,1)S(1)}, bf16[256,2048]{1,0:T(8,128)(2,1)}, u32[]{:S(2)}) copy-start(bf16[256,2048]{1,0:T(8,128)(2,1)} %get-tuple-element.43) | copy-start | bytes 3145732
  188.6 65.6 %collective-permute-start.2 = (bf16[256,2048]{1,0:T(8,128)(2,1)S(1)}, bf16[256,2048]{1,0:T(8,128)(2,1)S(1)}, u32[]{:S(2)}, u32[]{:S(2)}) collective-permute-start(bf16[256,2048]{1,0:T(8,128)(2,1)S(1)} %copy-done.4), channel_id=1, source_target_pairs={{0,12},{4,8},{8,4},{12,0},{1,13},{5,9},{9,5},{13,1},{2,14},{6,10},... | collective-permute-start | bytes 3145736 | tf_op jit(solution)/shard_map/ppermute | solution.py:112
  215.8 38.4 %copy-start.3 = (bf16[256,2048]{1,0:T(8,128)(2,1)S(1)}, bf16[256,2048]{1,0:T(8,128)(2,1)}, u32[]{:S(2)}) copy-start(bf16[256,2048]{1,0:T(8,128)(2,1)} %get-tuple-element.47) | copy-start | bytes 3145732
  257.0 10.5 %copy-start.21 = (s32[1,2048]{1,0:T(1,128)S(1)}, s32[1,2048]{1,0:T(1,128)}, u32[]{:S(2)}) copy-start(s32[1,2048]{1,0:T(1,128)} %copy-done.20) | copy-start | bytes 24580
  267.5 7.8 %copy-start.14 = (s32[1,2048]{1,0:T(1,128)S(1)}, s32[1,2048]{1,0:T(1,128)}, u32[]{:S(2)}) copy-start(s32[1,2048]{1,0:T(1,128)} %copy-done.13) | copy-start | bytes 24580
  267.6 7.8 %copy-start.26 = (bf16[2048,512]{0,1:T(8,128)(2,1)S(1)}, bf16[2048,512]{0,1:T(8,128)(2,1)}, u32[]{:S(2)}) copy-start(bf16[2048,512]{0,1:T(8,128)(2,1)} %all-reduce.4.cloned.1.call-done) | copy-start | bytes 6291460
  271.7 12.9 %collective-permute-start.10 = (bf16[256,512]{1,0:T(8,128)(2,1)S(1)}, bf16[256,512]{1,0:T(8,128)(2,1)S(1)}, u32[]{:S(2)}, u32[]{:S(2)}) collective-permute-start(bf16[256,512]{1,0:T(8,128)(2,1)S(1)} %get-tuple-element.53), channel_id=1, source_target_pairs={{0,8},{4,12},{8,0},{12,4},{1,9},{5,13},{9,1},{13,5},{2,10},{6,14},... | collective-permute-start | bytes 786440 | tf_op jit(solution)/shard_map/ppermute | solution.py:112
  272.4 13.8 %collective-permute-start.11 = (bf16[256,512]{1,0:T(8,128)(2,1)S(1)}, bf16[256,512]{1,0:T(8,128)(2,1)S(1)}, u32[]{:S(2)}, u32[]{:S(2)}) collective-permute-start(bf16[256,512]{1,0:T(8,128)(2,1)S(1)} %get-tuple-element.52), channel_id=1, source_target_pairs={{0,12},{4,8},{8,4},{12,0},{1,13},{5,9},{9,5},{13,1},{2,14},{6,10},... | collective-permute-start | bytes 786440 | tf_op jit(solution)/shard_map/ppermute | solution.py:112
  273.8 14.3 %collective-permute-start.9 = (bf16[256,512]{1,0:T(8,128)(2,1)S(1)}, bf16[256,512]{1,0:T(8,128)(2,1)S(1)}, u32[]{:S(2)}, u32[]{:S(2)}) collective-permute-start(bf16[256,512]{1,0:T(8,128)(2,1)S(1)} %get-tuple-element.54), channel_id=1, source_target_pairs={{0,4},{4,0},{8,12},{12,8},{1,5},{5,1},{9,13},{13,9},{2,6},{6,2},{1... | collective-permute-start | bytes 786440 | tf_op jit(solution)/shard_map/ppermute | solution.py:112
  277.8 16.0 %collective-permute-start.12 = (bf16[256,512]{1,0:T(8,128)(2,1)S(1)}, bf16[256,512]{1,0:T(8,128)(2,1)S(1)}, u32[]{:S(2)}, u32[]{:S(2)}) collective-permute-start(bf16[256,512]{1,0:T(8,128)(2,1)S(1)} %get-tuple-element.58), channel_id=1, source_target_pairs={{0,4},{4,0},{8,12},{12,8},{1,5},{5,1},{9,13},{13,9},{2,6},{6,2},{1... | collective-permute-start | bytes 786440 | tf_op jit(solution)/shard_map/ppermute | solution.py:112
  278.4 16.4 %collective-permute-start.13 = (bf16[256,512]{1,0:T(8,128)(2,1)S(1)}, bf16[256,512]{1,0:T(8,128)(2,1)S(1)}, u32[]{:S(2)}, u32[]{:S(2)}) collective-permute-start(bf16[256,512]{1,0:T(8,128)(2,1)S(1)} %get-tuple-element.57), channel_id=1, source_target_pairs={{0,8},{4,12},{8,0},{12,4},{1,9},{5,13},{9,1},{13,5},{2,10},{6,14},... | collective-permute-start | bytes 786440 | tf_op jit(solution)/shard_map/ppermute | solution.py:112
  284.6 14.9 %collective-permute-start.14 = (bf16[256,512]{1,0:T(8,128)(2,1)S(1)}, bf16[256,512]{1,0:T(8,128)(2,1)S(1)}, u32[]{:S(2)}, u32[]{:S(2)}) collective-permute-start(bf16[256,512]{1,0:T(8,128)(2,1)S(1)} %get-tuple-element.56), channel_id=1, source_target_pairs={{0,12},{4,8},{8,4},{12,0},{1,13},{5,9},{9,5},{13,1},{2,14},{6,10},... | collective-permute-start | bytes 786440 | tf_op jit(solution)/shard_map/ppermute | solution.py:112
  286.2 18.8 %collective-permute-start.15 = (bf16[256,512]{1,0:T(8,128)(2,1)S(1)}, bf16[256,512]{1,0:T(8,128)(2,1)S(1)}, u32[]{:S(2)}, u32[]{:S(2)}) collective-permute-start(bf16[256,512]{1,0:T(8,128)(2,1)S(1)} %get-tuple-element.62), channel_id=1, source_target_pairs={{0,4},{4,0},{8,12},{12,8},{1,5},{5,1},{9,13},{13,9},{2,6},{6,2},{1... | collective-permute-start | bytes 786440 | tf_op jit(solution)/shard_map/ppermute | solution.py:112
  288.1 18.4 %collective-permute-start.16 = (bf16[256,512]{1,0:T(8,128)(2,1)S(1)}, bf16[256,512]{1,0:T(8,128)(2,1)S(1)}, u32[]{:S(2)}, u32[]{:S(2)}) collective-permute-start(bf16[256,512]{1,0:T(8,128)(2,1)S(1)} %get-tuple-element.61), channel_id=1, source_target_pairs={{0,8},{4,12},{8,0},{12,4},{1,9},{5,13},{9,1},{13,5},{2,10},{6,14},... | collective-permute-start | bytes 786440 | tf_op jit(solution)/shard_map/ppermute | solution.py:112
  293.8 17.0 %collective-permute-start.17 = (bf16[256,512]{1,0:T(8,128)(2,1)S(1)}, bf16[256,512]{1,0:T(8,128)(2,1)S(1)}, u32[]{:S(2)}, u32[]{:S(2)}) collective-permute-start(bf16[256,512]{1,0:T(8,128)(2,1)S(1)} %get-tuple-element.60), channel_id=1, source_target_pairs={{0,12},{4,8},{8,4},{12,0},{1,13},{5,9},{9,5},{13,1},{2,14},{6,10},... | collective-permute-start | bytes 786440 | tf_op jit(solution)/shard_map/ppermute | solution.py:112
  294.8 20.7 %collective-permute-start.18 = (bf16[256,512]{1,0:T(8,128)(2,1)S(1)}, bf16[256,512]{1,0:T(8,128)(2,1)S(1)}, u32[]{:S(2)}, u32[]{:S(2)}) collective-permute-start(bf16[256,512]{1,0:T(8,128)(2,1)S(1)} %get-tuple-element.66), channel_id=1, source_target_pairs={{0,4},{4,0},{8,12},{12,8},{1,5},{5,1},{9,13},{13,9},{2,6},{6,2},{1... | collective-permute-start | bytes 786440 | tf_op jit(solution)/shard_map/ppermute | solution.py:112
  299.5 16.0 %collective-permute-start.19 = (bf16[256,512]{1,0:T(8,128)(2,1)S(1)}, bf16[256,512]{1,0:T(8,128)(2,1)S(1)}, u32[]{:S(2)}, u32[]{:S(2)}) collective-permute-start(bf16[256,512]{1,0:T(8,128)(2,1)S(1)} %get-tuple-element.65), channel_id=1, source_target_pairs={{0,8},{4,12},{8,0},{12,4},{1,9},{5,13},{9,1},{13,5},{2,10},{6,14},... | collective-permute-start | bytes 786440 | tf_op jit(solution)/shard_map/ppermute | solution.py:112
  305.0 13.3 %collective-permute-start.20 = (bf16[256,512]{1,0:T(8,128)(2,1)S(1)}, bf16[256,512]{1,0:T(8,128)(2,1)S(1)}, u32[]{:S(2)}, u32[]{:S(2)}) collective-permute-start(bf16[256,512]{1,0:T(8,128)(2,1)S(1)} %get-tuple-element.64), channel_id=1, source_target_pairs={{0,12},{4,8},{8,4},{12,0},{1,13},{5,9},{9,5},{13,1},{2,14},{6,10},... | collective-permute-start | bytes 786440 | tf_op jit(solution)/shard_map/ppermute | solution.py:112
  306.5 12.5 %copy-start.8 = (bf16[512,512]{1,0:T(8,128)(2,1)}, bf16[512,512]{1,0:T(8,128)(2,1)S(1)}, u32[]{:S(2)}) copy-start(bf16[512,512]{1,0:T(8,128)(2,1)S(1)} %fusion.180) | copy-start | bytes 1572868
  311.5 7.7 %copy-start.9 = (bf16[512,512]{1,0:T(8,128)(2,1)}, bf16[512,512]{1,0:T(8,128)(2,1)S(1)}, u32[]{:S(2)}) copy-start(bf16[512,512]{1,0:T(8,128)(2,1)S(1)} %fusion.179) | copy-start | bytes 1572868
  319.0 33.5 %copy-start.7 = (bf16[2,256,256]{2,1,0:T(8,128)(2,1)S(1)}, bf16[2,256,256]{2,1,0:T(8,128)(2,1)}, u32[]{:S(2)}) copy-start(bf16[2,256,256]{2,1,0:T(8,128)(2,1)} %param.5) | copy-start | bytes 786436
  319.2 48.8 %collective-permute-start.21 = (bf16[2048,512]{1,0:T(8,128)(2,1)S(1)}, bf16[2048,512]{1,0:T(8,128)(2,1)}, u32[]{:S(2)}, u32[]{:S(2)}) collective-permute-start(bf16[2048,512]{1,0:T(8,128)(2,1)S(1)} %pad_maximum_fusion.1), channel_id=1, source_target_pairs={{0,16},{16,0},{1,17},{17,1},{2,18},{18,2},{3,19},{19,3},{4,20},{20... | collective-permute-start | bytes 6291464 | tf_op jit(solution)/shard_map/ppermute | solution.py:161
  352.8 98.4 %all-to-all-start.2 = ((bf16[8,512,512]{2,1,0:T(8,128)(2,1)}), bf16[8,512,512]{2,1,0:T(8,128)(2,1)}, u32[]{:S(2)}, u32[]{:S(2)}) async-start(bf16[8,512,512]{2,1,0:T(8,128)(2,1)} %bitcast.132), calls=%async_computation.2 | async-start | bytes 8388608 | tf_op jit(solution)/shard_map/all_to_all | solution.py:121
  357.5 121.1 %all-reduce.6.cloned.1.call-start = ((), (), s32[]{:S(2)}) async-start(), calls=%async_computation.5 | async-start | bytes 4194304 | tf_op jit(solution)/shard_map/psum | solution.py:13
  357.6 10.5 %copy-start.15 = (s32[2048]{0:T(1024)S(1)}, s32[2048]{0:T(1024)}, u32[]{:S(2)}) copy-start(s32[2048]{0:T(1024)} %get-tuple-element.83) | copy-start | bytes 24580
  404.2 6.1 copy-start.18
  451.2 98.4 %all-to-all-start.1 = ((bf16[8,512,512]{2,1,0:T(8,128)(2,1)}), bf16[8,512,512]{2,1,0:T(8,128)(2,1)}, u32[]{:S(2)}, u32[]{:S(2)}) async-start(bf16[8,512,512]{2,1,0:T(8,128)(2,1)} %bitcast.131), calls=%async_computation.1 | async-start | bytes 8388608 | tf_op jit(solution)/shard_map/all_to_all | solution.py:121
  549.6 98.2 %all-to-all-start = ((bf16[8,512,512]{2,1,0:T(8,128)(2,1)}), bf16[8,512,512]{2,1,0:T(8,128)(2,1)}, u32[]{:S(2)}, u32[]{:S(2)}) async-start(bf16[8,512,512]{2,1,0:T(8,128)(2,1)} %bitcast.130), calls=%async_computation | async-start | bytes 8388608 | tf_op jit(solution)/shard_map/all_to_all | solution.py:121
  590.9 6.6 copy-start.23
  654.4 6.6 copy-start.22
  (10 other events, 34.3 us)
Sparse Core Ops, SparseCore 0:
  41.2 88.5 all-reduce.3
  391.3 69.8 all-reduce.5
